TPU v7x, 32 devices: a whole 2x2x4 slice. The times are simulated.
32 devices in a mesh: role: 2 (over core), dp: 8 (over z, x), head: 2 (over y).
Axes of the slice: x: 2, y: 2, z: 4, core: 2. Of those that a mesh axis runs over, the one named last changes fastest.
Arguments:
- layer_in: bfloat16 [2, 24576, 512], P('role', ('dp', 'head')), may hold values from -6 to 6
- lengths: int32 [2, 16, 24], P('role', 'dp'), may hold values from 1 to 100, 1536 in all within a row
- cotangent: bfloat16 [24576, 512], P(('dp', 'head')), may hold values from -6 to 6
- targets: int32 [24576], P(('dp', 'head')), may hold values 0 or 1
- self_qkv: bfloat16 [512, 3, 512], P(None, None, 'head'), may hold values from -0.25 to 0.25
- self_out: bfloat16 [512, 512], P('head'), may hold values from -1 to 1
- cross_q: bfloat16 [512, 512], P(None, 'head'), may hold values from -0.25 to 0.25
- cross_kv: bfloat16 [512, 2, 512], P(None, None, 'head'), may hold values from -0.25 to 0.25
- cross_out: bfloat16 [512, 512], P('head'), may hold values from -1 to 1
- ffn_in: bfloat16 [512, 2048], P(None, 'head'), may hold values from -0.25 to 0.25
- ffn_out: bfloat16 [2048, 512], P('head'), may hold values from -0.1875 to 0.1875
- norm_gain: float32 [3, 512], replicated, may hold values from 0.5 to 1.5
- norm_bias: float32 [3, 512], replicated, may hold values from -3 to 3
- halt_weight: float32 [512], replicated, may hold values from -0.25 to 0.25
- halt_bias: float32 [1], replicated, may hold values from -4 to 4
Outputs:
- layer_out: bfloat16 [2, 24576, 512], P('role', ('dp', 'head'))
- input_grads: float32 [2, 24576, 512], P('role', ('dp', 'head'))
- self_qkv_grad: float32 [512, 3, 512], P(None, None, 'head')
- self_out_grad: float32 [512, 512], P('head')
- cross_q_grad: float32 [512, 512], P(None, 'head')
- cross_kv_grad: float32 [512, 2, 512], P(None, None, 'head')
- cross_out_grad: float32 [512, 512], P('head')
- ffn_in_grad: float32 [512, 2048], P(None, 'head')
- ffn_out_grad: float32 [2048, 512], P('head')
- norm_gain_grad: float32 [3, 512], replicated
- norm_bias_grad: float32 [3, 512], replicated
- halt_weight_grad: float32 [512], replicated
- halt_bias_grad: float32 [1], replicated
Inputs may be any that keep to these rules, and one draw needn't show every extreme that they name: Row r of lengths[0] holds the 24 sentence lengths of source row r and row r of lengths[1] those of target row r; each row sums to 1536; target sentence c reads source sentence c of the same row. `targets`: 1 where the token halts.
All inputs are finite; a program needn't handle non-finite values. No bound on the sum of `targets` on one device may be relied on, other than what follows from the above.
Results may differ from a plain program's by a relative error of at most 0.017.
The roundings to bfloat16 on the way count: a program that leaves them out, or rounds other values in their place, can miss the bound.
Values may be sent and summed in bfloat16 or wider, within the bound.
No kernel may reach another device: no remote copies, remote signals or barrier semaphores. Data moves between devices by JAX's collectives and lax.ppermute only.
A program may use at most 192 MiB of HBM per device.

v0:
```python
import jax
import jax.numpy as jnp
from jax import lax
from jax.sharding import PartitionSpec as P

HEAD_DIM = 64
ROWS_DEV = 2
ROW_LEN = 1536


highest = lax.Precision.HIGHEST
masked_score = -1e30


def from_behind(value, axis, steps):
    count = lax.axis_size(axis)
    initial, last = (max(0, -steps), min(count, count - steps))
    return lax.ppermute(value, axis, [(source, source + steps) for source in range(initial, last)])


def norm_rows(values, norm_scale, shift_bias):
    center = values - jnp.mean(values, axis=-1, keepdims=True)
    spread = jnp.mean(center * center, axis=-1, keepdims=True)
    return center * lax.rsqrt(spread + 1e-05) * norm_scale + shift_bias


def segments(lengths_rows, row_len):
    sentence_ends = jnp.cumsum(lengths_rows, axis=-1)
    positions = jnp.arange(row_len, dtype=jnp.int32)
    return jnp.sum(
        (positions[None, :, None] >= sentence_ends[:, None, :]).astype(jnp.int32), axis=-1
    )


def allowed_keys(query_seg, key_seg, query_pos, causal):
    matches = query_seg[:, None] == key_seg[None, :]
    if causal:
        key_pos = jnp.arange(key_seg.shape[0], dtype=jnp.int32)
        matches = matches & (key_pos[None, :] <= query_pos[:, None])
    return matches


def attend_row(queries, key_rows, values, query_seg, key_seg, causal):
    row_len = queries.shape[0]
    block_rows = min(512, row_len)
    blocks = row_len // block_rows
    scaling = queries.shape[-1] ** (-0.5)
    positions = jnp.arange(row_len, dtype=jnp.int32).reshape(blocks, block_rows)

    def one_block(pieces):
        query_block, seg_block, pos_block = pieces
        scores = (
            jnp.einsum("qhe,khe->hqk", query_block, key_rows, preferred_element_type=jnp.float32)
            * scaling
        )
        allowed = allowed_keys(seg_block, key_seg, pos_block, causal)
        scores = jnp.where(allowed[None], scores, masked_score)
        row_max = jnp.max(scores, axis=-1, keepdims=True)
        weights = jnp.exp(scores - row_max)
        denominator = jnp.sum(weights, axis=-1, keepdims=True)
        probabilities = (weights / denominator).astype(jnp.bfloat16)
        mixture = jnp.einsum(
            "hqk,khe->qhe", probabilities, values, preferred_element_type=jnp.float32
        )
        return (mixture.astype(jnp.bfloat16), (row_max + jnp.log(denominator))[..., 0])

    shaped = queries.reshape((blocks, block_rows) + queries.shape[1:])
    mixture, log_sums = lax.map(
        one_block, (shaped, query_seg.reshape(blocks, block_rows), positions)
    )
    return (mixture.reshape(queries.shape), log_sums)


def attend_row_back(queries, key_rows, values, query_seg, key_seg, log_sums, out_grad, causal):
    row_len = queries.shape[0]
    block_rows = min(512, row_len)
    blocks = row_len // block_rows
    scaling = queries.shape[-1] ** (-0.5)
    positions = jnp.arange(row_len, dtype=jnp.int32).reshape(blocks, block_rows)

    def one_block(carry, pieces):
        key_grad, value_grad = carry
        query_block, seg_block, pos_block, sums_block, grad_block = pieces
        scores = (
            jnp.einsum("qhe,khe->hqk", query_block, key_rows, preferred_element_type=jnp.float32)
            * scaling
        )
        allowed = allowed_keys(seg_block, key_seg, pos_block, causal)
        probabilities = jnp.where(allowed[None], jnp.exp(scores - sums_block[..., None]), 0.0)
        prob_low = probabilities.astype(jnp.bfloat16)
        prob_grad = jnp.einsum(
            "qhe,khe->hqk", grad_block, values, preferred_element_type=jnp.float32
        )
        inner_sum = jnp.sum(probabilities * prob_grad, axis=-1, keepdims=True)
        score_grad = (probabilities * (prob_grad - inner_sum)).astype(jnp.bfloat16)
        query_grad = (
            jnp.einsum("hqk,khe->qhe", score_grad, key_rows, preferred_element_type=jnp.float32)
            * scaling
        )
        key_grad = (
            key_grad
            + jnp.einsum(
                "hqk,qhe->khe", score_grad, query_block, preferred_element_type=jnp.float32
            )
            * scaling
        )
        value_grad = value_grad + jnp.einsum(
            "hqk,qhe->khe", prob_low, grad_block, preferred_element_type=jnp.float32
        )
        return ((key_grad, value_grad), query_grad)

    start_grad = jnp.zeros(key_rows.shape, jnp.float32)
    shaped = queries.reshape((blocks, block_rows) + queries.shape[1:])
    grad_shaped = out_grad.reshape((blocks, block_rows) + out_grad.shape[1:])
    (key_grad, value_grad), query_grad = lax.scan(
        one_block,
        (start_grad, start_grad),
        (shaped, query_seg.reshape(blocks, block_rows), positions, log_sums, grad_shaped),
    )
    return (query_grad.reshape(queries.shape), key_grad, value_grad)


def rows_attend(queries, key_rows, values, query_seg, key_seg, causal):

    def per_row(pieces):
        return attend_row(*pieces, causal)

    return lax.map(per_row, (queries, key_rows, values, query_seg, key_seg))


def rows_attend_back(queries, key_rows, values, query_seg, key_seg, log_sums, out_grad, causal):

    def per_row(pieces):
        return attend_row_back(*pieces, causal)

    return lax.map(per_row, (queries, key_rows, values, query_seg, key_seg, log_sums, out_grad))


def gather_rows(values):
    return lax.all_gather(values, "head", axis=0, tiled=True)


def sum_rows(left, weight_rows):
    return lax.psum_scatter(
        jnp.dot(left, weight_rows, preferred_element_type=jnp.float32),
        "head",
        scatter_dimension=0,
        tiled=True,
    )


def keep_where(flag, value):
    return jnp.where(flag, value, jnp.zeros_like(value))


def shards(
    layer_in,
    lengths,
    cotangent,
    targets,
    self_qkv,
    self_out,
    cross_q,
    cross_kv,
    cross_out,
    ffn_in,
    ffn_out,
    norm_gain,
    norm_bias,
    halt_weight,
    halt_bias,
):
    decoder_side = lax.axis_index("role") == 1
    rows_here = layer_in[0]
    width = self_qkv.shape[0]
    qkv_used, self_out_used, cross_q_used, cross_kv_used = (self_qkv, self_out, cross_q, cross_kv)
    cross_out_used, ffn_in_used, ffn_out_used = (cross_out, ffn_in, ffn_out)
    local_rows = ROWS_DEV
    lengths_here = lengths[0]
    full_rows = local_rows * ROW_LEN
    heads_here = qkv_used.shape[2] // HEAD_DIM
    memory_rows, source_lengths = from_behind((rows_here, lengths_here), "role", 1)
    memory_full = gather_rows(memory_rows)
    pair_full = jnp.einsum(
        "td,dcf->tcf", memory_full, cross_kv_used, preferred_element_type=jnp.float32
    ).astype(jnp.bfloat16)
    source_lengths = jnp.where(decoder_side, source_lengths, lengths_here)
    target_seg = segments(lengths_here, ROW_LEN)
    source_seg = segments(source_lengths, ROW_LEN)
    states = rows_here.astype(jnp.float32)
    normed_one = norm_rows(states, norm_gain[0], norm_bias[0]).astype(jnp.bfloat16)
    normed_one_full = gather_rows(normed_one)
    triple = jnp.einsum(
        "td,dcf->tcf", normed_one_full, qkv_used, preferred_element_type=jnp.float32
    ).astype(jnp.bfloat16)
    triple_rows = triple.reshape(local_rows, ROW_LEN, 3, heads_here, HEAD_DIM)
    self_mix, self_sums = rows_attend(
        triple_rows[:, :, 0],
        triple_rows[:, :, 1],
        triple_rows[:, :, 2],
        target_seg,
        target_seg,
        True,
    )
    self_flat = self_mix.reshape(full_rows, -1)
    hidden = states + sum_rows(self_flat, self_out_used)
    normed_two = norm_rows(hidden, norm_gain[1], norm_bias[1]).astype(jnp.bfloat16)
    normed_two_full = gather_rows(normed_two)
    cross_query = jnp.dot(normed_two_full, cross_q_used, preferred_element_type=jnp.float32).astype(
        jnp.bfloat16
    )
    query_rows = cross_query.reshape(local_rows, ROW_LEN, heads_here, HEAD_DIM)
    pair_rows = pair_full.reshape(local_rows, ROW_LEN, 2, heads_here, HEAD_DIM)
    cross_mix, cross_sums = rows_attend(
        query_rows, pair_rows[:, :, 0], pair_rows[:, :, 1], target_seg, source_seg, False
    )
    cross_flat = cross_mix.reshape(full_rows, -1)
    hidden_two = hidden + sum_rows(cross_flat, cross_out_used)
    normed_three = norm_rows(hidden_two, norm_gain[2], norm_bias[2]).astype(jnp.bfloat16)
    normed_three_used = gather_rows(normed_three)
    inner = jnp.dot(normed_three_used, ffn_in_used, preferred_element_type=jnp.float32)
    activated = jax.nn.gelu(inner).astype(jnp.bfloat16)
    result = hidden_two + sum_rows(activated, ffn_out_used)
    logits = jnp.dot(result, halt_weight, precision=highest) + halt_bias[0]
    halt_grad = jax.nn.sigmoid(logits) - targets.astype(jnp.float32)
    out_grad = cotangent.astype(jnp.float32) + halt_grad[:, None] * halt_weight[None, :]
    halt_weight_grad = jnp.dot(halt_grad, result, precision=highest)
    halt_bias_grad = jnp.sum(halt_grad)[None]
    out_low = out_grad.astype(jnp.bfloat16)
    _, gelu_back = jax.vjp(jax.nn.gelu, inner)
    out_used = gather_rows(out_low)
    ffn_out_grad = jnp.einsum("tf,td->fd", activated, out_used, preferred_element_type=jnp.float32)
    act_grad = jnp.einsum("td,fd->tf", out_used, ffn_out_used, preferred_element_type=jnp.float32)
    inner_grad = gelu_back(act_grad)[0].astype(jnp.bfloat16)
    ffn_in_grad = jnp.einsum(
        "td,tf->df", normed_three_used, inner_grad, preferred_element_type=jnp.float32
    )
    normed_three_grad = sum_rows(inner_grad, ffn_in_used.T)
    _, norm_back_three = jax.vjp(norm_rows, hidden_two, norm_gain[2], norm_bias[2])
    state_part, gain_three, bias_three = norm_back_three(normed_three_grad)
    hidden_two_grad = out_grad + state_part
    cross_used = gather_rows(hidden_two_grad.astype(jnp.bfloat16))
    cross_out_grad = jnp.einsum(
        "tk,td->kd", cross_flat, cross_used, preferred_element_type=jnp.float32
    )
    cross_mix_grad = jnp.einsum(
        "td,kd->tk", cross_used, cross_out_used, preferred_element_type=jnp.float32
    ).astype(jnp.bfloat16)
    cross_mix_grad = cross_mix_grad.reshape(local_rows, ROW_LEN, heads_here, HEAD_DIM)
    query_grad, key_grad, value_grad = rows_attend_back(
        query_rows,
        pair_rows[:, :, 0],
        pair_rows[:, :, 1],
        target_seg,
        source_seg,
        cross_sums,
        cross_mix_grad,
        False,
    )
    query_low = query_grad.astype(jnp.bfloat16).reshape(full_rows, -1)
    pair_grad = (
        jnp.stack([key_grad, value_grad], axis=2).astype(jnp.bfloat16).reshape(full_rows, 2, -1)
    )
    cross_q_grad = jnp.einsum(
        "td,tf->df", normed_two_full, query_low, preferred_element_type=jnp.float32
    )
    normed_two_grad = sum_rows(query_low, cross_q_used.T)
    cross_kv_grad = jnp.einsum(
        "td,tcf->dcf", memory_full, pair_grad, preferred_element_type=jnp.float32
    )
    memory_part = sum_rows(pair_grad.reshape(full_rows, -1), cross_kv_used.reshape(width, -1).T)
    memory_grad = from_behind(memory_part.astype(jnp.bfloat16), "role", -1).astype(
        memory_part.dtype
    )
    _, norm_back_two = jax.vjp(norm_rows, hidden, norm_gain[1], norm_bias[1])
    state_part_two, gain_two, bias_two = norm_back_two(normed_two_grad)
    hidden_grad = hidden_two_grad + state_part_two
    self_used = gather_rows(hidden_grad.astype(jnp.bfloat16))
    self_out_grad = jnp.einsum(
        "tk,td->kd", self_flat, self_used, preferred_element_type=jnp.float32
    )
    self_mix_grad = jnp.einsum(
        "td,kd->tk", self_used, self_out_used, preferred_element_type=jnp.float32
    ).astype(jnp.bfloat16)
    self_mix_grad = self_mix_grad.reshape(local_rows, ROW_LEN, heads_here, HEAD_DIM)
    query_self_grad, key_self_grad, value_self_grad = rows_attend_back(
        triple_rows[:, :, 0],
        triple_rows[:, :, 1],
        triple_rows[:, :, 2],
        target_seg,
        target_seg,
        self_sums,
        self_mix_grad,
        True,
    )
    triple_grad = jnp.stack([query_self_grad, key_self_grad, value_self_grad], axis=2)
    triple_grad = triple_grad.astype(jnp.bfloat16).reshape(full_rows, 3, -1)
    self_qkv_grad = jnp.einsum(
        "td,tcf->dcf", normed_one_full, triple_grad, preferred_element_type=jnp.float32
    )
    normed_one_grad = sum_rows(triple_grad.reshape(full_rows, -1), qkv_used.reshape(width, -1).T)
    _, norm_back_one = jax.vjp(norm_rows, states, norm_gain[0], norm_bias[0])
    state_part_one, gain_one, bias_one = norm_back_one(normed_one_grad)
    state_grad = hidden_grad + state_part_one
    grads = (
        keep_where(decoder_side, self_qkv_grad),
        keep_where(decoder_side, self_out_grad),
        keep_where(decoder_side, cross_q_grad),
        keep_where(decoder_side, cross_kv_grad),
        keep_where(decoder_side, cross_out_grad),
        keep_where(decoder_side, ffn_in_grad),
        keep_where(decoder_side, ffn_out_grad),
    )
    side_grads = lax.psum(
        (grads[0], grads[1], grads[2], grads[3], grads[4], grads[5], grads[6]), "dp"
    )
    side_small = lax.psum(
        (
            keep_where(decoder_side, jnp.stack([gain_one, gain_two, gain_three])),
            keep_where(decoder_side, jnp.stack([bias_one, bias_two, bias_three])),
            keep_where(decoder_side, halt_weight_grad),
            keep_where(decoder_side, halt_bias_grad),
        ),
        ("dp", "head"),
    )
    totals = (
        lax.psum(side_grads[0].astype(jnp.bfloat16), "role").astype(jnp.float32),
        lax.psum(side_grads[1].astype(jnp.bfloat16), "role").astype(jnp.float32),
        lax.psum(side_grads[2].astype(jnp.bfloat16), "role").astype(jnp.float32),
        lax.psum(side_grads[3].astype(jnp.bfloat16), "role").astype(jnp.float32),
        lax.psum(side_grads[4].astype(jnp.bfloat16), "role").astype(jnp.float32),
        lax.psum(side_grads[5].astype(jnp.bfloat16), "role").astype(jnp.float32),
        lax.psum(side_grads[6].astype(jnp.bfloat16), "role").astype(jnp.float32),
        lax.psum(side_small[0].astype(jnp.bfloat16), "role").astype(jnp.float32),
        lax.psum(side_small[1].astype(jnp.bfloat16), "role").astype(jnp.float32),
        lax.psum(side_small[2].astype(jnp.bfloat16), "role").astype(jnp.float32),
        lax.psum(side_small[3].astype(jnp.bfloat16), "role").astype(jnp.float32),
    )
    layer_out = jnp.where(decoder_side, result.astype(jnp.bfloat16), rows_here)[None]
    input_grads = jnp.where(decoder_side, state_grad, memory_grad)[None]
    return (layer_out, input_grads) + tuple(totals)


def solution(mesh):
    placed = (
        P("role", ("dp", "head"), None),
        P("role", "dp", None),
        P(("dp", "head"), None),
        P(("dp", "head")),
        P(None, None, "head"),
        P("head", None),
        P(None, "head"),
        P(None, None, "head"),
        P("head", None),
        P(None, "head"),
        P("head", None),
        P(),
        P(),
        P(),
        P(),
    )
    return jax.shard_map(
        shards,
        mesh=mesh,
        in_specs=placed,
        out_specs=(
            P("role", ("dp", "head"), None),
            P("role", ("dp", "head"), None),
            P(None, None, "head"),
            P("head", None),
            P(None, "head"),
            P(None, None, "head"),
            P("head", None),
            P(None, "head"),
            P("head", None),
            P(),
            P(),
            P(),
            P(),
        ),
        check_vma=False,
    )
```

profile of v0, /device:TPU:0, one launch (start us, length us, event | category | flops | bytes accessed | tf_op | source)
XLA Modules:
  0.0 2023.0 jit_solution(1153979794120728135)
XLA Ops:
  17.4 47.4 %all-gather.8.cloned.1.call-done = bf16[3072,512]{1,0:T(8,128)(2,1)} async-done(((bf16[1536,512]{1,0:T(8,128)(2,1)}), bf16[3072,512]{1,0:T(8,128)(2,1)}) %all-gather.8.cloned.1.call-update) | async-done | bytes 3145744 | tf_op jit(solution)/shard_map/all_gather | solution.py:140
  101.9 87.4 %while.107 = (s32[]{:T(128)}, bf16[2,1536,4,64]{3,2,1,0:T(4,128)(2,1)}, f32[2,3,4,512]{3,2,1,0:T(4,128)S(1)}, bf16[2,1536,4,64]{1,3,2,0:T(8,128)(2,1)}, s32[2,15...) while((s32[]{:T(128)}, ...), condition=%wide.region_9.10_spmd, body=%wide.region_4.9_spmd.sunk | while | flops 845546496 | bytes 58098032 | solution.py:128
  108.3 34.7 %while.114 = (s32[]{:T(128)}, bf16[3,512,4,64]{1,3,2,0:T(8,128)(2,1)S(1)}, f32[3,4,512]{2,1,0:T(4,128)S(1)}, s32[3,512]{1,0:T(4,128)S(1)}, s32[1536]{0:T(1024)S(...) while((s32[]{:T(128)}, ...), condition=%wide.region_8.8_spmd, body=%wide.region_5.7_spmd.sunk | while | flops 845543424 | bytes 46221464 | solution.py:68
  152.0 34.7 %while.114 = (s32[]{:T(128)}, bf16[3,512,4,64]{1,3,2,0:T(8,128)(2,1)S(1)}, f32[3,4,512]{2,1,0:T(4,128)S(1)}, s32[3,512]{1,0:T(4,128)S(1)}, s32[1536]{0:T(1024)S(...) while((s32[]{:T(128)}, ...), condition=%wide.region_8.8_spmd, body=%wide.region_5.7_spmd.sunk | while | flops 845543424 | bytes 46221464 | solution.py:68
  204.6 70.9 %reduce-scatter.8.cloned.1.call-done = f32[1536,512]{1,0:T(8,128)} async-done(((f32[3072,512]{1,0:T(8,128)}), f32[1536,512]{1,0:T(8,128)}) %reduce-scatter.8.cloned.1.call-update) | async-done | bytes 3145744 | tf_op jit(solution)/shard_map/reduce_scatter | solution.py:144
  284.1 38.0 %all-gather.12.cloned.1.call-done = bf16[3072,512]{1,0:T(8,128)(2,1)} async-done(((bf16[1536,512]{1,0:T(8,128)(2,1)}), bf16[3072,512]{1,0:T(8,128)(2,1)}) %all-gather.12.cloned.1.call-update) | async-done | bytes 3145744 | tf_op jit(solution)/shard_map/all_gather | solution.py:140
  382.8 85.3 %while.109 = (s32[]{:T(128)}, bf16[2,1536,4,64]{3,2,1,0:T(4,128)(2,1)}, f32[2,3,4,512]{3,2,1,0:T(4,128)S(1)}, bf16[2,1536,4,64]{1,3,2,0:T(8,128)(2,1)}, s32[2,15...) while((s32[]{:T(128)}, ...), condition=%wide.region_20.21_spmd, body=%wide.region_15.20_spmd.sunk | while | flops 843970560 | bytes 58098024 | solution.py:128
  389.2 33.7 %while.115 = (s32[]{:T(128)}, bf16[3,512,4,64]{1,3,2,0:T(8,128)(2,1)S(1)}, f32[3,4,512]{2,1,0:T(4,128)S(1)}, s32[3,512]{1,0:T(4,128)S(1)}, s32[1536]{0:T(1024)S(...) while((s32[]{:T(128)}, ...), condition=%wide.region_19.19_spmd, body=%wide.region_16.18_spmd.sunk | while | flops 843970560 | bytes 46215312 | solution.py:68
  476.8 77.2 %reduce-scatter.10.cloned.1.call-done = f32[1536,512]{1,0:T(8,128)} async-done(((f32[3072,512]{1,0:T(8,128)}), f32[1536,512]{1,0:T(8,128)}) %reduce-scatter.10.cloned.1.call-update) | async-done | bytes 3145744 | tf_op jit(solution)/shard_map/reduce_scatter | solution.py:144
  560.7 45.0 %all-gather.14.cloned.1.call-done = bf16[3072,512]{1,0:T(8,128)(2,1)} async-done(((bf16[1536,512]{1,0:T(8,128)(2,1)}), bf16[3072,512]{1,0:T(8,128)(2,1)}) %all-gather.14.cloned.1.call-update) | async-done | bytes 3145744 | tf_op jit(solution)/shard_map/all_gather | solution.py:140
  625.1 76.4 %reduce-scatter.12.cloned.1.call-done = f32[1536,512]{1,0:T(8,128)} async-done(((f32[3072,512]{1,0:T(8,128)}), f32[1536,512]{1,0:T(8,128)}) %reduce-scatter.12.cloned.1.call-update) | async-done | bytes 3145744 | tf_op jit(solution)/shard_map/reduce_scatter | solution.py:144
  713.2 45.0 %all-gather.16.cloned.1.call-done = bf16[3072,512]{1,0:T(8,128)(2,1)} async-done(((bf16[1536,512]{1,0:T(8,128)(2,1)}), bf16[3072,512]{1,0:T(8,128)(2,1)}) %all-gather.16.cloned.1.call-update) | async-done | bytes 3145744 | tf_op jit(solution)/shard_map/all_gather | solution.py:140
  779.4 77.2 %reduce-scatter.14.cloned.1.call-done = f32[1536,512]{1,0:T(8,128)} async-done(((f32[3072,512]{1,0:T(8,128)}), f32[1536,512]{1,0:T(8,128)}) %reduce-scatter.14.cloned.1.call-update) | async-done | bytes 3145744 | tf_op jit(solution)/shard_map/reduce_scatter | solution.py:144
  865.5 45.0 %all-gather.18.cloned.1.call-done = bf16[3072,512]{1,0:T(8,128)(2,1)} async-done(((bf16[1536,512]{1,0:T(8,128)(2,1)}), bf16[3072,512]{1,0:T(8,128)(2,1)}) %all-gather.18.cloned.1.call-update) | async-done | bytes 3145744 | tf_op jit(solution)/shard_map/all_gather | solution.py:140
  925.2 180.1 %while.111 = (s32[]{:T(128)}, bf16[2,1536,4,64]{3,2,1,0:T(4,128)(2,1)}, bf16[2,1536,4,64]{1,3,2,0:T(8,128)(2,1)}, bf16[2,1536,4,64]{1,3,2,0:T(8,128)(2,1)}, bf16...) while((s32[]{:T(128)}, ...), condition=%wide.region_32.33_spmd, body=%wide.region_28.32_spmd.sunk | while | flops 2044459008 | bytes 198910896 | solution.py:136
  939.0 68.2 %while.116 = (s32[]{:T(128)}, f32[1536,4,64]{0,2,1:T(8,128)}, f32[1536,4,64]{0,2,1:T(8,128)}, bf16[3,512,4,64]{1,3,2,0:T(8,128)(2,1)}, bf16[3,512,4,64]{1,3,2,0:...) while((s32[]{:T(128)}, f32[1536,4,64]{0,2,1:T(8,128)}, ...), condition=%wide.region_31.31_spmd.clone, body=%wide.region_29.30_spmd.clone.sunk | while | flops 2044459008 | bytes 143970608 | solution.py:115
  1028.8 68.2 %while.116 = (s32[]{:T(128)}, f32[1536,4,64]{0,2,1:T(8,128)}, f32[1536,4,64]{0,2,1:T(8,128)}, bf16[3,512,4,64]{1,3,2,0:T(8,128)(2,1)}, bf16[3,512,4,64]{1,3,2,0:...) while((s32[]{:T(128)}, f32[1536,4,64]{0,2,1:T(8,128)}, ...), condition=%wide.region_31.31_spmd.clone, body=%wide.region_29.30_spmd.clone.sunk | while | flops 2044459008 | bytes 143970608 | solution.py:115
  1116.2 75.1 %reduce-scatter.16.cloned.1.call-done = f32[1536,512]{1,0:T(8,128)} async-done(((f32[3072,512]{1,0:T(8,128)}), f32[1536,512]{1,0:T(8,128)}) %reduce-scatter.16.cloned.1.call-update) | async-done | bytes 3145744 | tf_op jit(solution)/shard_map/reduce_scatter | solution.py:144
  1268.1 180.4 %while.113 = (s32[]{:T(128)}, bf16[2,1536,4,64]{1,3,2,0:T(8,128)(2,1)}, bf16[2,1536,4,64]{1,3,2,0:T(8,128)(2,1)}, bf16[2,1536,4,64]{1,3,2,0:T(8,128)(2,1)}, bf16...) while((s32[]{:T(128)}, ...), condition=%wide.region_40.41_spmd, body=%wide.region_36.40_spmd.sunk | while | flops 2046034944 | bytes 174039744 | solution.py:136
  1282.4 68.4 %while.117 = (s32[]{:T(128)}, f32[1536,4,64]{0,2,1:T(8,128)}, f32[1536,4,64]{0,2,1:T(8,128)}, bf16[3,512,4,64]{1,3,2,0:T(8,128)(2,1)}, bf16[3,512,4,64]{1,3,2,0:...) while((s32[]{:T(128)}, f32[1536,4,64]{0,2,1:T(8,128)}, ...), condition=%wide.region_39.39_spmd.clone, body=%wide.region_37.38_spmd.clone.sunk | while | flops 2046031872 | bytes 143976768 | solution.py:115
  1372.5 68.3 %while.117 = (s32[]{:T(128)}, f32[1536,4,64]{0,2,1:T(8,128)}, f32[1536,4,64]{0,2,1:T(8,128)}, bf16[3,512,4,64]{1,3,2,0:T(8,128)(2,1)}, bf16[3,512,4,64]{1,3,2,0:...) while((s32[]{:T(128)}, f32[1536,4,64]{0,2,1:T(8,128)}, ...), condition=%wide.region_39.39_spmd.clone, body=%wide.region_37.38_spmd.clone.sunk | while | flops 2046031872 | bytes 143976768 | solution.py:115
  1488.4 326.4 %all-reduce.8 = (bf16[512,2,256]{0,2,1:T(8,128)(2,1)}, bf16[512,3,256]{2,0,1:T(8,128)(2,1)}, bf16[256,512]{1,0:T(8,128)(2,1)}, bf16[512,256]{1,0:T(8,128)(2,1)},...) all-reduce(f32[512,2,256]{0,2,1:T(8,128)} %fusion.120, ...), channel_id=1, replica_groups=mesh['role'=2,'dp'=8,'head'=2] {'dp'}, use_global_device_ids=true, to_apply=%region_51.52 | all-reduce | flops 2097152 | bytes 12582912 | tf_op jit(solution)/shard_map/psum | solution.py:314
  1859.6 62.9 %reduce-scatter.18.cloned.1.call-done = f32[1536,512]{1,0:T(8,128)} async-done(((f32[3072,512]{1,0:T(8,128)}), f32[1536,512]{1,0:T(8,128)}) %reduce-scatter.18.cloned.1.call-update) | async-done | bytes 3145744 | tf_op jit(solution)/shard_map/reduce_scatter | solution.py:144
  1927.5 76.4 %all-reduce = (bf16[3,512]{1,0:T(4,128)(2,1)S(1)}, bf16[3,512]{1,0:T(4,128)(2,1)S(1)}, bf16[512]{0:T(512)(128)(2,1)S(1)}, bf16[1]{0:T(256)(128)(2,1)}) all-reduce(f32[3,512]{1,0:T(4,128)S(1)} %get-tuple-element.951, f32[3,512]{1,0:T(4,128)S(1)} %get-tuple-element.952, ...), channel_id=1, replica_groups=mesh['role'=2,'dp'=8,'head'=2] {'dp','head'}, use_global_device_ids=true, to_apply=%region_62.63 | all-reduce | flops 3585 | bytes 21510 | tf_op jit(solution)/shard_map/psum | solution.py:317
  (837 shorter events, 972.3 us)
Async XLA Ops:
  7.2 598.5 %copy-start = (bf16[512,1024]{1,0:T(8,128)(2,1)S(1)}, bf16[512,1024]{1,0:T(8,128)(2,1)}, u32[]{:S(2)}) copy-start(bf16[512,1024]{1,0:T(8,128)(2,1)} %param.40) | copy-start | bytes 3145732
  7.2 57.6 %all-gather.8.cloned.1.call-start = ((), (), s32[]{:S(2)}) async-start(), calls=%async_computation.7 | async-start | bytes 4718592 | tf_op jit(solution)/shard_map/all_gather | solution.py:140
  17.0 258.4 %reduce-scatter.8.cloned.1.call-start = ((), (), s32[]{:S(2)}) async-start(), calls=%async_computation.8 | async-start | bytes 9437184 | tf_op jit(solution)/shard_map/reduce_scatter | solution.py:144
  198.2 123.8 %all-gather.12.cloned.1.call-start = ((), (), s32[]{:S(2)}) async-start(), calls=%async_computation.10 | async-start | bytes 4718592 | tf_op jit(solution)/shard_map/all_gather | solution.py:140
  199.6 4.9 collective-permute-start
  204.5 164.5 %all-gather.10.cloned.1.call-start = ((), (), s32[]{:S(2)}) async-start(), calls=%async_computation.9 | async-start | bytes 4718592 | tf_op jit(solution)/shard_map/all_gather | solution.py:140
  281.1 272.8 %reduce-scatter.10.cloned.1.call-start = ((), (), s32[]{:S(2)}) async-start(), calls=%async_computation.11 | async-start | bytes 9437184 | tf_op jit(solution)/shard_map/reduce_scatter | solution.py:144
  281.2 2.5 collective-permute-start.1
  476.8 128.9 %all-gather.14.cloned.1.call-start = ((), (), s32[]{:S(2)}) async-start(), calls=%async_computation.12 | async-start | bytes 4718592 | tf_op jit(solution)/shard_map/all_gather | solution.py:140
  560.6 140.9 %reduce-scatter.12.cloned.1.call-start = ((), (), s32[]{:S(2)}) async-start(), calls=%async_computation.13 | async-start | bytes 9437184 | tf_op jit(solution)/shard_map/reduce_scatter | solution.py:144
  624.3 134.0 %all-gather.16.cloned.1.call-start = ((), (), s32[]{:S(2)}) async-start(), calls=%async_computation.14 | async-start | bytes 4718592 | tf_op jit(solution)/shard_map/all_gather | solution.py:140
  625.1 83.0 %copy-start.90 = (f32[512]{0:T(512)S(1)}, f32[512]{0:T(512)}, u32[]{:S(2)}) copy-start(f32[512]{0:T(512)} %param.44) | copy-start | bytes 6148
  711.6 150.2 %copy-start.73 = (f32[1536]{0:T(1024)}, f32[1536]{0:T(1024)S(1)}, u32[]{:S(2)}) copy-start(f32[1536]{0:T(1024)S(1)} %get-tuple-element.903) | copy-start | bytes 18436
  713.2 143.4 %reduce-scatter.14.cloned.1.call-start = ((), (), s32[]{:S(2)}) async-start(), calls=%async_computation.15 | async-start | bytes 9437184 | tf_op jit(solution)/shard_map/reduce_scatter | solution.py:144
  779.3 131.2 %all-gather.18.cloned.1.call-start = ((), (), s32[]{:S(2)}) async-start(), calls=%async_computation.16 | async-start | bytes 4718592 | tf_op jit(solution)/shard_map/all_gather | solution.py:140
  865.4 325.9 %reduce-scatter.16.cloned.1.call-start = ((), (), s32[]{:S(2)}) async-start(), calls=%async_computation.17 | async-start | bytes 9437184 | tf_op jit(solution)/shard_map/reduce_scatter | solution.py:144
  1114.0 77.3 %copy-start.77 = (f32[1536]{0:T(1024)S(1)}, f32[1536]{0:T(1024)}, u32[]{:S(2)}) copy-start(f32[1536]{0:T(1024)} %copy-done.76) | copy-start | bytes 18436
  1114.0 77.3 %copy-start.81 = (f32[1536]{0:T(1024)S(1)}, f32[1536]{0:T(1024)}, u32[]{:S(2)}) copy-start(f32[1536]{0:T(1024)} %copy-done.80) | copy-start | bytes 18436
  1114.1 137.1 %all-gather.20.cloned.1.call-start = ((), (), s32[]{:S(2)}) async-start(), calls=%async_computation.18 | async-start | bytes 4718592 | tf_op jit(solution)/shard_map/all_gather | solution.py:140
  1116.2 78.6 %copy-start.87 = (f32[1536]{0:T(1024)S(1)}, f32[1536]{0:T(1024)}, u32[]{:S(2)}) copy-start(f32[1536]{0:T(1024)} %copy-done.86) | copy-start | bytes 18436
  1200.0 643.3 %reduce-scatter.20.cloned.1.call-start = ((), (), s32[]{:S(2)}) async-start(), calls=%async_computation.20 | async-start | bytes 9437184 | tf_op jit(solution)/shard_map/reduce_scatter | solution.py:144
  1251.1 596.9 %all-reduce.7.cloned.1.call-start = ((), (), s32[]{:S(2)}) async-start(), calls=%async_computation.21 | async-start | bytes 8388608 | tf_op jit(solution)/shard_map/psum | solution.py:330
  1814.8 107.7 %reduce-scatter.18.cloned.1.call-start = ((), (), s32[]{:S(2)}) async-start(), calls=%async_computation.19 | async-start | bytes 9437184 | tf_op jit(solution)/shard_map/reduce_scatter | solution.py:144
  1846.7 162.8 %collective-permute-start.2 = (bf16[1536,512]{1,0:T(8,128)(2,1)}, bf16[1536,512]{1,0:T(8,128)(2,1)}, u32[]{:S(2)}, u32[]{:S(2)}) collective-permute-start(bf16[1536,512]{1,0:T(8,128)(2,1)} %convert_element_type.208), channel_id=1, source_target_pairs={{16,0},{17,1},{18,2},{19,3},{20,4},{21,5},{22,6},{23,7},{24,8},{25... | collective-permute-start | bytes 4718600 | tf_op jit(solution)/shard_map/ppermute | solution.py:18
  (179 other events, 1449.9 us)
Sparse Core Ops, SparseCore 0:
  17.2 47.6 all-gather.7
  198.4 77.0 reduce-scatter.7
  277.1 44.9 all-gather.11
  324.1 44.9 all-gather.9
  476.9 77.0 reduce-scatter.9
  560.7 44.9 all-gather.13
  624.4 77.0 reduce-scatter.11
  713.3 44.9 all-gather.15
  779.5 77.0 reduce-scatter.13
  865.6 44.9 all-gather.17
  1114.2 77.0 reduce-scatter.15
  1200.2 44.9 all-gather.19
  1251.2 77.2 reduce-scatter.19
  1814.9 26.9 all-reduce.6
  1844.1 78.2 reduce-scatter.17
where the time goes:
time: 2030 us; the launch traced here: 2020 us
  waiting for transfers between devices  685 us (34%)
  matrix products  421 us (21%)
  blocking collectives  406 us (20%)
  local copies, waits for them, and re-layouts  312 us (15%)
  other arithmetic  170 us (8%)
    reduce_scatter x7, waiting for transfers between devices, sum_rows(): lax.psum_scatter(jnp.dot(left, weight_rows, preferred_element_type=jnp.fl...  440 us
    psum x1, blocking collectives, shards(): lax.psum((grads[0], grads[1], grads[2], grads[3], grads[4], grads[5], gra...  326 us
    all_gather x7, waiting for transfers between devices, gather_rows(): return lax.all_gather(values, 'head', axis=0, tiled=True)  242 us
    dot_general x24, matrix products, one_block(): jnp.einsum('qhe,khe->hqk', query_block, key_rows, preferred_element_type=...  95 us
    psum x1, blocking collectives, shards(): lax.psum((keep_where(decoder_side, jnp.stack([gain_one, gain_two, gain_th...  76.4 us
    dot_general x12, matrix products, one_block(): jnp.einsum('hqk,khe->qhe', probabilities, values, preferred_element_type=...  55.3 us
    dot_general x12, matrix products, one_block(): jnp.einsum('hqk,qhe->khe', score_grad, query_block, preferred_element_typ...  48.4 us
    dot_general x12, matrix products, one_block(): jnp.einsum('hqk,qhe->khe', prob_low, grad_block, preferred_element_type=j...  46.3 us
  transfers between devices with their start and end apart: 18, of which 14 were waited for; matrix products, arithmetic and copies ran while one was open for 18% of the time, Pallas kernels for 0%

commit v1 on v0

v1 whole, which is shorter than its diff:
```python
import functools

import jax
import jax.numpy as jnp
from jax import lax
from jax.experimental import pallas as pl
from jax.experimental.pallas import tpu as pltpu
from jax.sharding import PartitionSpec as P

F32 = jnp.float32
BF16 = jnp.bfloat16

HEAD_DIM = 64
HALF = 256
HEADS = HALF // HEAD_DIM
HALO = 128
WINDOW = 128
MASKED = -1e30
VMEM_LIMIT = 56 * 1024 * 1024
ANY = pl.BlockSpec(memory_space=pl.ANY)
VMEM = pl.BlockSpec(memory_space=pltpu.VMEM)
SMEM = pl.BlockSpec(memory_space=pltpu.SMEM)
ARRIVALS = (0, 2, 1, 3)


def dot(a, b):
    return jnp.dot(a, b, preferred_element_type=F32)


def dot_nt(a, b):
    return lax.dot_general(a, b, (((1,), (1,)), ((), ())), preferred_element_type=F32)


def dot_tn(a, b):
    return lax.dot_general(a, b, (((0,), (0,)), ((), ())), preferred_element_type=F32)


def norm_parts(values):
    center = values - jnp.mean(values, axis=-1, keepdims=True)
    spread = jnp.mean(center * center, axis=-1, keepdims=True)
    scale = lax.rsqrt(spread + 1e-05)
    return center * scale, scale


def norm_back(grad, hat, scale, gain):
    grad_hat = grad * gain
    first = jnp.mean(grad_hat, axis=-1, keepdims=True)
    second = jnp.mean(grad_hat * hat, axis=-1, keepdims=True)
    return scale * (grad_hat - first - hat * second)


def start_weights(meta, own, arrived, held, sem):
    copies = [pltpu.make_async_copy(own, held.at[pl.ds(0, 4)], sem.at[0])]
    for at, (ref, flip) in enumerate(zip(arrived, ARRIVALS)):
        copies.append(pltpu.make_async_copy(ref, held.at[4 + (meta[1] ^ flip)], sem.at[1 + at]))
    for copy in copies:
        copy.start()
    return copies


def put_grads(meta, grads, keep, send, sem):
    rows = keep.shape[3]
    copies = []
    for half in range(2):
        for rel in range(4):
            at = 4 * half + (rel ^ meta[1])
            for z in range(4):
                first = pl.multiple_of((z ^ meta[2]) * rows, rows)
                target = (send if rel & 1 else keep).at[half, rel >> 1, z]
                copy = pltpu.make_async_copy(grads.at[at, pl.ds(first, rows)], target, sem.at[0])
                copy.start()
                copies.append(copy)
    return copies


def sentence_range(meta, segs, rows_here):
    first_row = meta[0] * rows_here

    def step(c, carry):
        target, source, low, high = carry
        target_end = target + segs[1, c]
        source_end = source + segs[0, c]
        mine = (target_end > first_row) & (target < first_row + rows_here)
        low = jnp.where(mine, jnp.minimum(low, source), low)
        high = jnp.where(mine, jnp.maximum(high, source_end), high)
        return target_end, source_end, low, high

    zero = jnp.int32(0)
    _, _, low, high = lax.fori_loop(0, segs.shape[1], step, (zero, zero, jnp.int32(1 << 20), zero))
    return low, high


def each_sentence(meta, segs, rows_here, body):
    first_row = meta[0] * rows_here

    def step(c, carry):
        target, source = carry
        target_end = target + segs[1, c]
        source_end = source + segs[0, c]

        @pl.when((target_end > first_row) & (target < first_row + rows_here))
        def _():
            shift = HALO - first_row
            body(target + shift, target_end + shift, source, source_end)

        return target_end, source_end

    lax.fori_loop(0, segs.shape[1], step, (jnp.int32(0), jnp.int32(0)))


def window_of(start):
    return pl.multiple_of((start // 16) * 16, 16)


def head_lanes():
    return lax.broadcasted_iota(jnp.int32, (1, HALF), 1) // HEAD_DIM


def spread_heads(block):
    lanes = head_lanes()
    return jnp.concatenate(
        [jnp.where(lanes == h, block, jnp.zeros_like(block)) for h in range(HEADS)], axis=0
    )


def join_heads(stacked):
    lanes = head_lanes()
    rows = stacked.shape[0] // HEADS
    total = jnp.zeros((rows, HALF), F32)
    for h in range(HEADS):
        total = jnp.where(lanes == h, stacked[h * rows : (h + 1) * rows], total)
    return total


def allowed_window(query_axis, q_first, q_low, q_high, k_first, k_low, k_high, causal):
    shape = (WINDOW, WINDOW)
    q = lax.broadcasted_iota(jnp.int32, shape, query_axis) + q_first
    k = lax.broadcasted_iota(jnp.int32, shape, 1 - query_axis) + k_first
    ok = (q >= q_low) & (q < q_high) & (k >= k_low) & (k < k_high)
    if causal:
        ok = ok & (k <= q)
    return ok


def attend_window(q, k, v, allowed):
    scale = jnp.asarray(HEAD_DIM**-0.5, BF16)
    scores = dot_nt(spread_heads(q * scale), k)
    allowed = jnp.concatenate([allowed] * HEADS, axis=0)
    scores = jnp.where(allowed, scores, MASKED)
    weights = jnp.exp(scores - jnp.max(scores, axis=-1, keepdims=True))
    inverse = 1.0 / jnp.sum(weights, axis=-1, keepdims=True)
    probabilities = jnp.where(allowed, weights * inverse, 0.0).astype(BF16)
    return join_heads(dot(probabilities, v))


def attend_window_back(q, k, v, grad, allowed):
    scale = HEAD_DIM**-0.5
    q_heads = spread_heads(q * jnp.asarray(scale, BF16))
    grad_heads = spread_heads(grad)
    allowed = jnp.concatenate([allowed] * HEADS, axis=1)
    scores = jnp.where(allowed, dot_nt(k, q_heads), MASKED)
    weights = jnp.exp(scores - jnp.max(scores, axis=0, keepdims=True))
    inverse = 1.0 / jnp.sum(weights, axis=0, keepdims=True)
    probabilities = jnp.where(allowed, weights * inverse, 0.0)
    prob_grad = dot_nt(v, grad_heads)
    inner = jnp.sum(probabilities * prob_grad, axis=0, keepdims=True)
    score_grad = (probabilities * (prob_grad - inner)).astype(BF16)
    q_grad = join_heads(dot_tn(score_grad, k)) * scale
    k_grad = dot(score_grad, q_heads)
    v_grad = dot(probabilities.astype(BF16), grad_heads)
    return q_grad, k_grad, v_grad


def out_product(mixes, held):
    left = sum(dot(mix, held[4 * half + 3, 0:HALF]) for half, mix in enumerate(mixes))
    right = sum(dot(mix, held[4 * half + 3, HALF:]) for half, mix in enumerate(mixes))
    return jnp.concatenate([left, right], axis=1)


def out_grads(grad_low, held, mixes, mix_grads, grads, first):
    rows = grad_low.shape[0]
    for half in range(2):
        at = 4 * half + 3
        for lo in range(0, rows, HALF):
            block = grad_low[lo : lo + HALF]
            mix_grad = dot_nt(block[:, :HALF], held[at, 0:HALF]) + dot_nt(
                block[:, HALF:], held[at, HALF:]
            )
            mix_grads[half, first + lo : first + lo + HALF] = mix_grad.astype(BF16)
        mix = mixes[half]
        grads[at, 0:HALF] = dot_tn(mix, grad_low[:, :HALF]).astype(BF16)
        grads[at, HALF:] = dot_tn(mix, grad_low[:, HALF:]).astype(BF16)


def copy_by_role(meta, pairs_zero, pairs_one, sem):
    @pl.when(meta[0] == 0)
    def _():
        for source, target in pairs_zero:
            pltpu.make_async_copy(source, target, sem).start()

    @pl.when(meta[0] == 1)
    def _():
        for source, target in pairs_one:
            pltpu.make_async_copy(source, target, sem).start()


def wait_by_role(meta, pairs_zero, pairs_one, sem):
    @pl.when(meta[0] == 0)
    def _():
        for source, target in pairs_zero:
            pltpu.make_async_copy(source, target, sem).wait()

    @pl.when(meta[0] == 1)
    def _():
        for source, target in pairs_one:
            pltpu.make_async_copy(source, target, sem).wait()


def states_copies(rows_ref, other_ref, held, here):
    zero = [(other_ref.at[pl.ds(0, here)], held.at[pl.ds(HALO, here)])]
    one = [(rows_ref.at[pl.ds(here - HALO, here + HALO)], held.at[pl.ds(0, here + HALO)])]
    return zero, one


def self_forward(
    meta, segs, rows_ref, other_ref, gain, bias, own, w1, w2, w3, w4,
    hidden, mix, qkv, held, states, mixed, sem_w, sem_x,
):
    here = hidden.shape[0]
    full = here + HALO
    state_copies = states_copies(rows_ref, other_ref, states, here)
    copy_by_role(meta, *state_copies, sem_x)
    weights = start_weights(meta, own, (w1, w2, w3, w4), held, sem_w)
    qkv[:, :, full:] = jnp.zeros((2, 3, WINDOW, HALF), BF16)
    mixed[...] = jnp.zeros(mixed.shape, F32)
    wait_by_role(meta, *state_copies, sem_x)

    @pl.when(meta[0] == 0)
    def _():
        states[0:HALO] = jnp.zeros((HALO, states.shape[1]), BF16)

    for copy in weights:
        copy.wait()
    step = full // 2
    for lo in range(0, full, step):
        hat, _ = norm_parts(states[lo : lo + step].astype(F32))
        normed = (hat * gain[0:1] + bias[0:1]).astype(BF16)
        for half in range(2):
            for c in range(3):
                qkv[half, c, lo : lo + step] = dot(normed, held[4 * half + c]).astype(BF16)

    def sentence(low, high, _low, _high):
        first = window_of(low)
        allowed = allowed_window(
            0, first, jnp.maximum(low, HALO), jnp.minimum(high, full), first, low, high, True
        )
        at = pl.ds(first, WINDOW)
        for half in range(2):
            mixed[half, at] += attend_window(qkv[half, 0, at], qkv[half, 1, at], qkv[half, 2, at], allowed)

    each_sentence(meta, segs, here, sentence)
    mix[...] = mixed[:, HALO:full].astype(BF16)
    for lo in range(0, here, HALF):
        at = slice(lo, lo + HALF)
        hidden[at] = states[HALO + lo : HALO + lo + HALF].astype(F32) + out_product(
            [mix[0, at], mix[1, at]], held
        )


def memory_copies(rows_ref, other_ref, held):
    return [(rows_ref, held)], [(other_ref, held)]


def cross_forward(
    meta, segs, rows_ref, other_ref, hidden, gain, bias, own, w1, w2, w3, w4,
    hidden_two, mix, queries, pairs, held, memory, mixed, sem_w, sem_x,
):
    here = hidden.shape[0]
    full = here + HALO
    copies = memory_copies(rows_ref, other_ref, memory)
    copy_by_role(meta, *copies, sem_x)
    weights = start_weights(meta, own, (w1, w2, w3, w4), held, sem_w)
    queries[:, 0:HALO] = jnp.zeros((2, HALO, HALF), BF16)
    queries[:, full:] = jnp.zeros((2, WINDOW, HALF), BF16)
    mixed[...] = jnp.zeros(mixed.shape, F32)
    pairs[...] = jnp.zeros(pairs.shape, BF16)
    low, high = sentence_range(meta, segs, here)
    wait_by_role(meta, *copies, sem_x)
    for copy in weights:
        copy.wait()

    def project(block, _):
        at = pl.ds(pl.multiple_of(block * HALF, HALF), HALF)
        for half in range(2):
            for c in range(2):
                pairs[half, c, at] = dot(memory[at], held[4 * half + 1 + c]).astype(BF16)
        return 0

    lax.fori_loop(low // HALF, (high + HALF - 1) // HALF, project, 0)
    for lo in range(0, here, HALF):
        hat, _ = norm_parts(hidden[lo : lo + HALF])
        normed = (hat * gain[1:2] + bias[1:2]).astype(BF16)
        for half in range(2):
            queries[half, HALO + lo : HALO + lo + HALF] = dot(normed, held[4 * half]).astype(BF16)

    def sentence(low, high, source_low, source_high):
        first = window_of(low)
        source_first = window_of(source_low)
        allowed = allowed_window(
            0, first, jnp.maximum(low, HALO), jnp.minimum(high, full),
            source_first, source_low, source_high, False,
        )
        at = pl.ds(first, WINDOW)
        source_at = pl.ds(source_first, WINDOW)
        for half in range(2):
            mixed[half, at] += attend_window(
                queries[half, at], pairs[half, 0, source_at], pairs[half, 1, source_at], allowed
            )

    each_sentence(meta, segs, here, sentence)
    mix[...] = mixed[:, HALO:full].astype(BF16)
    for lo in range(0, here, HALF):
        at = slice(lo, lo + HALF)
        hidden_two[at] = hidden[at] + out_product([mix[0, at], mix[1, at]], held)


def gelu_both(inner):
    rate = 0.7978845608028654
    square = inner * inner
    bent = jnp.tanh(rate * inner * (1.0 + 0.044715 * square))
    half = 0.5 * (1.0 + bent)
    slope = half + 0.5 * inner * (1.0 - bent * bent) * (rate * (1.0 + 3 * 0.044715 * square))
    return inner * half, slope


def feed_forward(
    meta, hidden_two, cotangent, targets, gain, bias, halt_weight, halt_bias,
    own_in, i1, i2, i3, i4, own_out, o1, o2, o3, o4,
    result_low, hidden_grad, small, keep_in, send_in, keep_out, send_out,
    held_in, held_out, normed, active, slopes, total, out_low, cot, tgt, grads_in, grads_out,
    sem_w, sem_o, sem_x, sem_g,
):
    here = hidden_two.shape[0]
    first = pl.multiple_of(meta[0] * here, here)
    cot_copy = pltpu.make_async_copy(cotangent.at[pl.ds(first, here)], cot, sem_x.at[0])
    tgt_copy = pltpu.make_async_copy(targets.at[pl.ds(first, here)], tgt, sem_x.at[1])
    weights = start_weights(meta, own_in, (i1, i2, i3, i4), held_in, sem_w)
    weights += start_weights(meta, own_out, (o1, o2, o3, o4), held_out, sem_o)
    cot_copy.start()
    tgt_copy.start()
    blocks = [slice(lo, lo + HALF) for lo in range(0, here, HALF)]
    for at in blocks:
        hat, _ = norm_parts(hidden_two[at])
        normed[at] = (hat * gain[2:3] + bias[2:3]).astype(BF16)
        total[at] = hidden_two[at]
    for copy in weights:
        copy.wait()

    def forward(j, _):
        for at in blocks:
            value, slope = gelu_both(dot(normed[at], held_in[j]))
            value = value.astype(BF16)
            active[j, at] = value
            slopes[j, at] = slope
            total[at] += dot(value, held_out[j])
        return 0

    lax.fori_loop(0, 8, forward, 0)
    cot_copy.wait()
    tgt_copy.wait()
    weight_sum = jnp.zeros((1, halt_weight.shape[1]), F32)
    bias_sum = jnp.zeros((1, 1), F32)
    for at in blocks:
        result = total[at]
        result_low[at] = result.astype(BF16)
        logits = jnp.sum(result * halt_weight[...], axis=-1, keepdims=True) + halt_bias[0]
        halt_grad = 1.0 / (1.0 + jnp.exp(-logits)) - tgt[at]
        out_grad = cot[at].astype(F32) + halt_grad * halt_weight[...]
        out_low[at] = out_grad.astype(BF16)
        hidden_grad[at] = out_grad
        total[at] = jnp.zeros((HALF, result.shape[1]), F32)
        weight_sum += jnp.sum(halt_grad * result, axis=0, keepdims=True)
        bias_sum += jnp.sum(halt_grad, axis=0, keepdims=True)

    def backward(j, _):
        inner_grads = []
        for at in blocks:
            inner_grad = (dot_nt(out_low[at], held_out[j]) * slopes[j, at]).astype(BF16)
            inner_grads.append(inner_grad)
            total[at] += dot_nt(inner_grad, held_in[j])
        grads_in[j] = dot_tn(normed[...], jnp.concatenate(inner_grads, axis=0)).astype(BF16)
        grads_out[j] = dot_tn(active[j], out_low[...]).astype(BF16)
        return 0

    lax.fori_loop(0, 8, backward, 0)
    copies = put_grads(meta, grads_in, keep_in, send_in, sem_g)
    copies += put_grads(meta, grads_out, keep_out, send_out, sem_g)
    gain_sum = jnp.zeros_like(weight_sum)
    shift_sum = jnp.zeros_like(weight_sum)
    for at in blocks:
        hat, scale = norm_parts(hidden_two[at])
        grad = total[at]
        hidden_grad[at] += norm_back(grad, hat, scale, gain[2:3])
        gain_sum += jnp.sum(grad * hat, axis=0, keepdims=True)
        shift_sum += jnp.sum(grad, axis=0, keepdims=True)
    small[...] = jnp.concatenate(
        [gain_sum, shift_sum, weight_sum, jnp.broadcast_to(bias_sum, weight_sum.shape)], axis=0
    )
    for copy in copies:
        copy.wait()


def cross_backward(
    meta, segs, rows_ref, other_ref, hidden, upper_grad, mix, queries, pairs, gain, bias,
    own, w1, w2, w3, w4,
    lower_grad, memory_grad, small, keep, send,
    held, memory, mix_grads, q_grad, pair_grads, pair_sums, grads, sem_w, sem_x, sem_g,
):
    here, width = hidden.shape
    full = here + HALO
    copies = memory_copies(rows_ref, other_ref, memory)
    copy_by_role(meta, *copies, sem_x)
    weights = start_weights(meta, own, (w1, w2, w3, w4), held, sem_w)
    mix_grads[:, 0:HALO] = jnp.zeros((2, HALO, HALF), BF16)
    mix_grads[:, full:] = jnp.zeros((2, WINDOW, HALF), BF16)
    q_grad[...] = jnp.zeros(q_grad.shape, F32)
    pair_grads[...] = jnp.zeros(pair_grads.shape, F32)
    pair_sums[...] = jnp.zeros(pair_sums.shape, F32)
    memory_grad[...] = jnp.zeros(memory_grad.shape, BF16)
    source_low, source_high = sentence_range(meta, segs, here)
    for copy in weights:
        copy.wait()
    out_grads(upper_grad[...].astype(BF16), held, [mix[0], mix[1]], mix_grads, grads, HALO)

    def sentence(low, high, source_low, source_high):
        first = window_of(low)
        source_first = window_of(source_low)
        allowed = allowed_window(
            1, first, jnp.maximum(low, HALO), jnp.minimum(high, full),
            source_first, source_low, source_high, False,
        )
        at = pl.ds(first, WINDOW)
        source_at = pl.ds(source_first, WINDOW)
        for half in range(2):
            dq, dk, dv = attend_window_back(
                queries[half, at], pairs[half, 0, source_at], pairs[half, 1, source_at],
                mix_grads[half, at], allowed,
            )
            q_grad[half, at] += dq
            pair_grads[half, 0, source_at] += dk
            pair_grads[half, 1, source_at] += dv

    each_sentence(meta, segs, here, sentence)
    wait_by_role(meta, *copies, sem_x)

    def project(block, _):
        at = pl.ds(pl.multiple_of(block * HALF, HALF), HALF)
        row_grad = jnp.zeros((HALF, width), F32)
        for half in range(2):
            for c in range(2):
                low = pair_grads[half, c, at].astype(BF16)
                row_grad += dot_nt(low, held[4 * half + 1 + c])
                pair_sums[half, c] += dot_tn(memory[at], low)
        memory_grad[at] = row_grad.astype(BF16)
        return 0

    lax.fori_loop(source_low // HALF, (source_high + HALF - 1) // HALF, project, 0)
    for half in range(2):
        for c in range(2):
            grads[4 * half + 1 + c] = pair_sums[half, c].astype(BF16)
    gain_sum = jnp.zeros((1, width), F32)
    shift_sum = jnp.zeros((1, width), F32)
    normed = []
    q_low = [q_grad[half, HALO:full].astype(BF16) for half in range(2)]
    for lo in range(0, here, HALF):
        at = slice(lo, lo + HALF)
        hat, scale = norm_parts(hidden[at])
        normed.append((hat * gain[1:2] + bias[1:2]).astype(BF16))
        grad = dot_nt(q_low[0][at], held[0]) + dot_nt(q_low[1][at], held[4])
        lower_grad[at] = upper_grad[at] + norm_back(grad, hat, scale, gain[1:2])
        gain_sum += jnp.sum(grad * hat, axis=0, keepdims=True)
        shift_sum += jnp.sum(grad, axis=0, keepdims=True)
    normed = jnp.concatenate(normed, axis=0)
    for half in range(2):
        grads[4 * half] = dot_tn(normed, q_low[half]).astype(BF16)
    put = put_grads(meta, grads, keep, send, sem_g)
    small[...] = jnp.concatenate([gain_sum, shift_sum], axis=0)
    for copy in put:
        copy.wait()


def self_backward(
    meta, segs, rows_ref, other_ref, upper_grad, mix, qkv, gain, bias, own, w1, w2, w3, w4,
    state_grad, halo_grad, small, keep, send,
    held, states, mix_grads, qkv_grads, grads, sem_w, sem_x, sem_g,
):
    here, width = upper_grad.shape
    full = here + HALO
    state_copies = states_copies(rows_ref, other_ref, states, here)
    copy_by_role(meta, *state_copies, sem_x)
    weights = start_weights(meta, own, (w1, w2, w3, w4), held, sem_w)
    mix_grads[:, 0:HALO] = jnp.zeros((2, HALO, HALF), BF16)
    mix_grads[:, full:] = jnp.zeros((2, WINDOW, HALF), BF16)
    qkv_grads[...] = jnp.zeros(qkv_grads.shape, F32)
    wait_by_role(meta, *state_copies, sem_x)

    @pl.when(meta[0] == 0)
    def _():
        states[0:HALO] = jnp.zeros((HALO, width), BF16)

    for copy in weights:
        copy.wait()
    out_grads(upper_grad[...].astype(BF16), held, [mix[0], mix[1]], mix_grads, grads, HALO)

    def sentence(low, high, _low, _high):
        first = window_of(low)
        allowed = allowed_window(
            1, first, jnp.maximum(low, HALO), jnp.minimum(high, full), first, low, high, True
        )
        at = pl.ds(first, WINDOW)
        for half in range(2):
            back = attend_window_back(
                qkv[half, 0, at], qkv[half, 1, at], qkv[half, 2, at], mix_grads[half, at], allowed
            )
            for c in range(3):
                qkv_grads[half, c, at] += back[c]

    each_sentence(meta, segs, here, sentence)
    gain_sum = jnp.zeros((1, width), F32)
    shift_sum = jnp.zeros((1, width), F32)
    normed = []
    step = full // 2
    for lo in range(0, full, step):
        at = slice(lo, lo + step)
        hat, scale = norm_parts(states[at].astype(F32))
        normed.append((hat * gain[0:1] + bias[0:1]).astype(BF16))
        grad = jnp.zeros((step, width), F32)
        for half in range(2):
            for c in range(3):
                grad += dot_nt(qkv_grads[half, c, at].astype(BF16), held[4 * half + c])
        back = norm_back(grad, hat, scale, gain[0:1])
        if lo == 0:
            halo_grad[...] = back[:HALO]
            state_grad[0 : step - HALO] = upper_grad[0 : step - HALO] + back[HALO:]
        else:
            state_grad[lo - HALO :] = upper_grad[lo - HALO :] + back
        gain_sum += jnp.sum(grad * hat, axis=0, keepdims=True)
        shift_sum += jnp.sum(grad, axis=0, keepdims=True)
    normed = jnp.concatenate(normed, axis=0)
    for half in range(2):
        for c in range(3):
            grads[4 * half + c] = dot_tn(normed, qkv_grads[half, c, 0:full].astype(BF16)).astype(BF16)
    put = put_grads(meta, grads, keep, send, sem_g)
    small[...] = jnp.concatenate([gain_sum, shift_sum], axis=0)
    for copy in put:
        copy.wait()


def unpack(kind, meta, mine, by_x, by_role, by_both, *rest):
    outs, (held, sem) = rest[:-2], rest[-2:]
    rows = mine.shape[1]
    copies = []
    for rel, ref in ((0, mine), (2, by_x), (1, by_role), (3, by_both)):
        for z in range(4):
            first = pl.multiple_of((z ^ meta[2]) * rows, rows)
            copy = pltpu.make_async_copy(
                ref.at[z], held.at[rel ^ meta[1], pl.ds(first, rows)], sem.at[0]
            )
            copy.start()
            copies.append(copy)
    for copy in copies:
        copy.wait()
    if kind == "rows":
        for j in range(4):
            outs[0][j * 4 * rows : (j + 1) * 4 * rows] = held[j].astype(F32)
        return
    if kind == "columns":
        for j in range(4):
            outs[0][:, j * HALF : (j + 1) * HALF] = held[j].astype(F32)
        return
    at = 0
    for out in outs[:-1]:
        for c in range(out.shape[1] // HALF):
            out[:, c * HALF : (c + 1) * HALF] = held[at].astype(F32)
            at += 1
    outs[-1][:, 0:HALF] = held[3, 0:HALF].astype(F32)
    outs[-1][:, HALF:] = held[3, HALF:].astype(F32)


def shape(*dims, dtype=F32):
    return jax.ShapeDtypeStruct(dims, dtype)


def call(body, outs, out_specs, scratch, flops, name, in_specs):
    return pl.pallas_call(
        body,
        out_shape=outs,
        in_specs=in_specs,
        out_specs=out_specs,
        scratch_shapes=scratch,
        name=name,
        compiler_params=pltpu.CompilerParams(vmem_limit_bytes=VMEM_LIMIT),
        cost_estimate=pl.CostEstimate(flops=flops, bytes_accessed=10_000_000, transcendentals=0),
    )


def flip(value, axis, bit=1):
    count = lax.axis_size(axis)
    return lax.ppermute(value, axis, [(i, i ^ bit) for i in range(count)])


def add(a, b):
    return (a.astype(F32) + b.astype(F32)).astype(BF16)


def fetch_other(own, me):
    first = flip(lax.dynamic_index_in_dim(own, me, 0, keepdims=False), "head")
    second = flip(first, "dp", 1)
    return own, first, second, flip(first, "role"), flip(second, "role")


def reduce_sum(keep, send):
    got = flip(send, "role")
    away, near = add(keep[1], got[1]), add(keep[0], got[0])
    got = flip(away, "head")
    away, near = add(near[1], got[1]), add(near[0], got[0])
    got = flip(away, "dp", 1)
    away, near = add(near[2:], got[2:]), add(near[:2], got[:2])
    got = flip(away, "dp", 2)
    away, near = add(near[1], got[1]), add(near[0], got[0])
    total = add(near, flip(away, "dp", 4))
    bit = 8
    while bit < lax.axis_size("dp"):
        total = add(total, flip(total, "dp", bit))
        bit *= 2
    return total


def spread_sum(total):
    beside = flip(total, "dp", 4)
    mine = jnp.stack([total, beside, flip(total, "dp", 2), flip(beside, "dp", 2)])
    by_x = flip(mine, "dp", 1)
    return mine, by_x, flip(mine, "role"), flip(by_x, "role")


def all_sum(value):
    value = value + flip(value, "role")
    value = value + flip(value, "head")
    bit = 1
    while bit < lax.axis_size("dp"):
        value = value + flip(value, "dp", bit)
        bit *= 2
    return value


def shards(
    layer_in,
    lengths,
    cotangent,
    targets,
    self_qkv,
    self_out,
    cross_q,
    cross_kv,
    cross_out,
    ffn_in,
    ffn_out,
    norm_gain,
    norm_bias,
    halt_weight,
    halt_bias,
):
    role, head, place = (lax.axis_index(name) for name in ("role", "head", "dp"))
    target_side = role == 1
    me = 2 * (place & 1) + role
    z_me = (place & 2) + ((place >> 2) & 1)
    meta = jnp.stack([role, me, z_me, head]).astype(jnp.int32)
    rows = layer_in[0]
    row_len, width = rows.shape
    here = row_len // 2
    full = here + HALO

    other_rows = flip(rows, "role")
    lens = lax.dynamic_index_in_dim(lengths[0], head, 0, keepdims=False)
    other_lens = flip(lens, "role")
    segs = jnp.where(target_side, jnp.stack([other_lens, lens]), jnp.stack([lens, other_lens]))

    def halves(out):
        return jnp.concatenate([out[:, :HALF], out[:, HALF:]], axis=0)[None]

    self_own = jnp.concatenate([self_qkv.transpose(1, 0, 2), halves(self_out)], axis=0)
    cross_own = jnp.concatenate(
        [cross_q[None], cross_kv.transpose(1, 0, 2), halves(cross_out)], axis=0
    )
    in_own = ffn_in.reshape(width, 4, HALF).transpose(1, 0, 2)
    out_own = ffn_out.reshape(4, HALF, width)
    self_weights = fetch_other(self_own, me)
    cross_weights = fetch_other(cross_own, me)
    in_weights = fetch_other(in_own, me)
    out_weights = fetch_other(out_own, me)

    weight_specs = [ANY] * 5
    held = pltpu.VMEM((8, width, HALF), BF16)
    weight_sems = pltpu.SemaphoreType.DMA((5,))
    one_sem = pltpu.SemaphoreType.DMA
    dense = 2 * here * width * HALF * 8

    hidden, self_mix, qkv = call(
        self_forward,
        (shape(here, width), shape(2, here, HALF, dtype=BF16), shape(2, 3, full + WINDOW, HALF, dtype=BF16)),
        (VMEM,) * 3,
        [held, pltpu.VMEM((full, width), BF16), pltpu.VMEM((2, full + WINDOW, HALF), F32), weight_sems, one_sem],
        2 * dense,
        "self_forward",
        [SMEM, SMEM, ANY, ANY, VMEM, VMEM] + weight_specs,
    )(meta, segs, rows, other_rows, norm_gain, norm_bias, *self_weights)

    hidden_two, cross_mix, queries, pairs = call(
        cross_forward,
        (
            shape(here, width),
            shape(2, here, HALF, dtype=BF16),
            shape(2, full + WINDOW, HALF, dtype=BF16),
            shape(2, 2, row_len + WINDOW, HALF, dtype=BF16),
        ),
        (VMEM,) * 4,
        [held, pltpu.VMEM((row_len, width), BF16), pltpu.VMEM((2, full + WINDOW, HALF), F32), weight_sems, one_sem],
        2 * dense,
        "cross_forward",
        [SMEM, SMEM, ANY, ANY, VMEM, VMEM, VMEM] + weight_specs,
    )(meta, segs, rows, other_rows, hidden, norm_gain, norm_bias, *cross_weights)

    grad_parts = shape(2, 2, 4, width // 4, HALF, dtype=BF16)
    out_parts = shape(2, 2, 4, HALF // 4, width, dtype=BF16)
    grad_sems = pltpu.SemaphoreType.DMA((1,))
    result_low, two_grad, ffn_small, keep_in, send_in, keep_out, send_out = call(
        feed_forward,
        (shape(here, width, dtype=BF16), shape(here, width), shape(4, width), grad_parts, grad_parts, out_parts, out_parts),
        (VMEM, VMEM, VMEM, ANY, ANY, ANY, ANY),
        [
            held,
            pltpu.VMEM((8, HALF, width), BF16),
            pltpu.VMEM((here, width), BF16),
            pltpu.VMEM((8, here, HALF), BF16),
            pltpu.VMEM((8, here, HALF), F32),
            pltpu.VMEM((here, width), F32),
            pltpu.VMEM((here, width), BF16),
            pltpu.VMEM((here, width), BF16),
            pltpu.VMEM((here, 1), F32),
            pltpu.VMEM((8, width, HALF), BF16),
            pltpu.VMEM((8, HALF, width), BF16),
            weight_sems,
            weight_sems,
            pltpu.SemaphoreType.DMA((2,)),
            grad_sems,
        ],
        6 * dense,
        "feed_forward",
        [SMEM, VMEM, ANY, ANY, VMEM, VMEM, VMEM, SMEM] + weight_specs * 2,
    )(
        meta, hidden_two, cotangent, targets.astype(F32)[:, None], norm_gain, norm_bias,
        halt_weight[None], halt_bias, *in_weights, *out_weights,
    )

    one_grad, memory_part, cross_small, keep_cross, send_cross = call(
        cross_backward,
        (shape(here, width), shape(row_len, width, dtype=BF16), shape(2, width), grad_parts, grad_parts),
        (VMEM, VMEM, VMEM, ANY, ANY),
        [
            held,
            pltpu.VMEM((row_len, width), BF16),
            pltpu.VMEM((2, full + WINDOW, HALF), BF16),
            pltpu.VMEM((2, full + WINDOW, HALF), F32),
            pltpu.VMEM((2, 2, row_len + WINDOW, HALF), F32),
            pltpu.VMEM((2, 2, width, HALF), F32),
            pltpu.VMEM((8, width, HALF), BF16),
            weight_sems,
            one_sem,
            grad_sems,
        ],
        4 * dense,
        "cross_backward",
        [SMEM, SMEM, ANY, ANY] + [VMEM] * 7 + weight_specs,
    )(
        meta, segs, rows, other_rows, hidden, two_grad, cross_mix, queries, pairs, norm_gain, norm_bias,
        *cross_weights,
    )

    state_grad, halo_grad, self_small, keep_self, send_self = call(
        self_backward,
        (shape(here, width), shape(HALO, width), shape(2, width), grad_parts, grad_parts),
        (VMEM, VMEM, VMEM, ANY, ANY),
        [
            held,
            pltpu.VMEM((full, width), BF16),
            pltpu.VMEM((2, full + WINDOW, HALF), BF16),
            pltpu.VMEM((2, 3, full + WINDOW, HALF), F32),
            pltpu.VMEM((8, width, HALF), BF16),
            weight_sems,
            one_sem,
            grad_sems,
        ],
        4 * dense,
        "self_backward",
        [SMEM, SMEM, ANY, ANY] + [VMEM] * 5 + weight_specs,
    )(
        meta, segs, rows, other_rows, one_grad, self_mix, qkv, norm_gain, norm_bias, *self_weights,
    )

    def totals(kind, keep, send, out_shapes):
        pieces = spread_sum(reduce_sum(keep, send))
        rows_each = keep.shape[3]
        return call(
            functools.partial(unpack, kind),
            out_shapes,
            (VMEM,) * len(out_shapes),
            [pltpu.VMEM((4, 4 * rows_each, keep.shape[4]), BF16), pltpu.SemaphoreType.DMA((1,))],
            0,
            "unpack_" + kind,
            [SMEM] + [ANY] * 4,
        )(meta, *pieces)

    (ffn_out_grad,) = totals("rows", keep_out, send_out, (shape(4 * HALF, width),))
    (ffn_in_grad,) = totals("columns", keep_in, send_in, (shape(width, 4 * HALF),))
    cross_q_grad, cross_kv_grad, cross_out_grad = totals(
        "mixed", keep_cross, send_cross, (shape(width, HALF), shape(width, 2 * HALF), shape(HALF, width))
    )
    self_qkv_grad, self_out_grad = totals(
        "mixed", keep_self, send_self, (shape(width, 3 * HALF), shape(HALF, width))
    )

    small = all_sum(
        jnp.concatenate(
            [
                self_small[0:1], cross_small[0:1], ffn_small[0:1],
                self_small[1:2], cross_small[1:2], ffn_small[1:2], ffn_small[2:4],
            ],
            axis=0,
        )
    )

    to_target, to_memory = [(0, 1)], [(1, 0)]
    low_result = lax.ppermute(result_low, "role", to_target)
    low_grad = lax.ppermute(state_grad.astype(BF16), "role", to_target).astype(F32)
    other_memory = lax.ppermute(memory_part, "role", to_memory)
    layer_out = jnp.where(
        target_side, jnp.concatenate([low_result, result_low], axis=0), rows
    )[None]
    halo_rows = jnp.concatenate(
        [jnp.zeros((here - HALO, width), F32), halo_grad, jnp.zeros((here, width), F32)], axis=0
    )
    target_grads = jnp.concatenate([low_grad, state_grad], axis=0) + halo_rows
    memory_grads = memory_part.astype(F32) + other_memory.astype(F32)
    input_grads = jnp.where(target_side, target_grads, memory_grads)[None]
    return (
        layer_out,
        input_grads,
        self_qkv_grad.reshape(width, 3, HALF),
        self_out_grad,
        cross_q_grad,
        cross_kv_grad.reshape(width, 2, HALF),
        cross_out_grad,
        ffn_in_grad,
        ffn_out_grad,
        small[0:3],
        small[3:6],
        small[6],
        small[7, 0:1],
    )


def solution(mesh):
    placed = (
        P("role", ("dp", "head"), None),
        P("role", "dp", None),
        P(("dp", "head"), None),
        P(("dp", "head")),
        P(None, None, "head"),
        P("head", None),
        P(None, "head"),
        P(None, None, "head"),
        P("head", None),
        P(None, "head"),
        P("head", None),
        P(),
        P(),
        P(),
        P(),
    )
    return jax.shard_map(
        shards,
        mesh=mesh,
        in_specs=placed,
        out_specs=(
            P("role", ("dp", "head"), None),
            P("role", ("dp", "head"), None),
            P(None, None, "head"),
            P("head", None),
            P(None, "head"),
            P(None, None, "head"),
            P("head", None),
            P(None, "head"),
            P("head", None),
            P(),
            P(),
            P(),
            P(),
        ),
        check_vma=False,
    )
```

time: 2030 us -> 349 us (0.17)
  waiting for transfers between devices: 685 us -> 86.7 us
  matrix products: 421 us -> 0 us
  blocking collectives: 406 us -> 0 us
  local copies, waits for them, and re-layouts: 312 us -> 19.1 us
  other arithmetic: 170 us -> 17 us
  Pallas kernels: 0 us -> 140 us
  starting transfers between devices: 6.52 us -> 80.7 us
    reduce_scatter x7 -> x0, waiting for transfers between devices: 440 us -> none  [sum_rows(): lax.psum_scatter(jnp.dot(left, weight_rows, preferred_element_type=jnp.fl...]
    dot_general x107 -> x0, matrix products: 421 us -> none  [the longest x24 95 us: one_block(): jnp.einsum('qhe,khe->hqk', query_block, key_rows, preferred_element_type=...]
    psum x3 -> x0, blocking collectives: 406 us -> none  [the longest x1 326 us: shards(): lax.psum((grads[0], grads[1], grads[2], grads[3], grads[4], grads[5], gra...]
    all_gather x7 -> x0, waiting for transfers between devices: 242 us -> none  [gather_rows(): return lax.all_gather(values, 'head', axis=0, tiled=True)]
    pallas_call x0 -> x9, Pallas kernels: none -> 140 us  [the longest x1 29.1 us: shards(): call(cross_backward, (shape(here, width), shape(row_len, width, dtype=BF1...]
    ppermute x3 -> x70, waiting for transfers between devices: 2.81 us -> 86.7 us  [the longest x67 86.6 us: flip(): return lax.ppermute(value, axis, [(i, i ^ bit) for i in range(count)])]
    ppermute x3 -> x70, starting transfers between devices: 5.9 us -> 80.7 us  [the longest x67 76.5 us: flip(): return lax.ppermute(value, axis, [(i, i ^ bit) for i in range(count)])]
    reshape x28 -> x2, local copies, waits for them, and re-layouts: 74.6 us -> 4.15 us  [the longest x1 2.85 us: shards(): cross_kv_grad.reshape(width, 2, HALF)]
  transfers between devices with their start and end apart: 18 -> 70, of which waited for: 14 -> 29; matrix products, arithmetic and copies ran while one was open for 18% -> 10% of each run, Pallas kernels for 0% -> 32%
where the time goes in v1:
time: 349 us; the launch traced here: 346 us
  Pallas kernels  140 us (40%)
  waiting for transfers between devices  86.7 us (25%)
  starting transfers between devices  80.7 us (23%)
  local copies, waits for them, and re-layouts  19.1 us (5%)
  other arithmetic  17 us (5%)
    ppermute x67, waiting for transfers between devices, flip(): return lax.ppermute(value, axis, [(i, i ^ bit) for i in range(count)])  86.6 us
    ppermute x67, starting transfers between devices, flip(): return lax.ppermute(value, axis, [(i, i ^ bit) for i in range(count)])  76.5 us
    pallas_call x1, Pallas kernels, shards(): call(cross_backward, (shape(here, width), shape(row_len, width, dtype=BF1...  29.1 us
    pallas_call x1, Pallas kernels, shards(): call(self_backward, (shape(here, width), shape(HALO, width), shape(2, wid...  26.6 us
    pallas_call x1, Pallas kernels, shards(): call(feed_forward, (shape(here, width, dtype=BF16), shape(here, width), s...  25.1 us
    pallas_call x1, Pallas kernels, shards(): call(cross_forward, (shape(here, width), shape(2, here, HALF, dtype=BF16)...  23.8 us
    pallas_call x1, Pallas kernels, shards(): call(self_forward, (shape(here, width), shape(2, here, HALF, dtype=BF16),...  22.3 us
    pallas_call x4, Pallas kernels, totals(): call(functools.partial(unpack, kind), out_shapes, (VMEM,) * len(out_shape...  13.4 us
  transfers between devices with their start and end apart: 70, of which 29 were waited for; matrix products, arithmetic and copies ran while one was open for 10% of the time, Pallas kernels for 32%

profile of v1, /device:TPU:0, one launch (start us, length us, event | category | flops | bytes accessed | tf_op | source)
XLA Modules:
  0.0 346.2 jit_solution(3178133522279349779)
XLA Ops:
  18.8 5.5 %collective-permute-done.10.i1 = bf16[512,256]{1,0:T(8,128)(2,1)S(1)} collective-permute-done((bf16[512,256]{1,0:T(8,128)(2,1)}, bf16[512,256]{1,0:T(8,128)(2,1)S(1)}, u32[]{:S(2)}, u32[]{:S(2)}) %collective-permute-start.10) | collective-permute-done | bytes 262176 | tf_op jit(solution)/shard_map/ppermute | solution.py:609
  34.4 22.3 %self_forward.1 = (f32[768,512]{1,0:T(8,128)}, bf16[2,768,256]{2,1,0:T(8,128)(2,1)}, bf16[2,3,1024,256]{3,2,1,0:T(8,128)(2,1)}) custom-call(s32[4]{0:T(128)} %pad_add_fusion.meta, s32[2,24]{1,0:T(2,128)} %add_select_fusion.segs, bf16[1536,512]{1,0:T(8,128)(2,1)} %bitcast.184, bf16[1536,512]{1,0:T(8,128)(2,1)} %collective-permute-done.1.other_ref, ...), custom_call_target="tpu_custom_call" | custom-call | flops 3221225472 | bytes 10000000 | tf_op jit(solution)/shard_map/self_forward/pallas_call | solution.py:708
  58.1 23.8 %cross_forward.1 = (f32[768,512]{1,0:T(8,128)}, bf16[2,768,256]{2,1,0:T(8,128)(2,1)}, bf16[2,1024,256]{2,1,0:T(8,128)(2,1)}, bf16[2,2,1664,256]{3,2,1,0:T(8,128)(2,1)}) custom-call(s32[4]{0:T(128)} %pad_add_fusion.meta, s32[2,24]{1,0:T(2,128)} %add_select_fusion.segs, bf16[1536,512]{1,0:T(8,128)(2,1)} %bitcast.185, ...), custom_call_target="tpu_custom_call" | custom-call | flops 3221225472 | bytes 10000000 | tf_op jit(solution)/shard_map/cross_forward/pallas_call | solution.py:718
  83.0 25.1 %feed_forward.1 = (bf16[768,512]{1,0:T(8,128)(2,1)}, f32[768,512]{1,0:T(8,128)}, f32[4,512]{1,0:T(4,128)}, bf16[2,2,4,128,256]{4,3,2,1,0:T(8,128)(2,1)}, bf16[2,...) custom-call(s32[4]{0:T(128)} %pad_add_fusion.meta, ...), custom_call_target="tpu_custom_call" | custom-call | flops 9663676416 | bytes 10000000 | tf_op jit(solution)/shard_map/feed_forward/pallas_call | solution.py:736
  108.6 29.1 %cross_backward.1 = (f32[768,512]{1,0:T(8,128)}, bf16[1536,512]{1,0:T(8,128)(2,1)}, f32[2,512]{1,0:T(2,128)}, bf16[2,2,4,128,256]{4,3,2,1,0:T(8,128)(2,1)}, bf16[2,2,4,128,256]{4,3,2,1,0:T(8,128)(2,1)}) custom-call(s32[4]{0:T(128)} %pad_add_fusion.meta, s32[2,24]{1,0:T(2,128)} %add_select_fusion.segs, bf16[1536,512]{1,0:T(8,128)(2,1)} %bitcast.186, ...), custom_call_target="tpu_custom_call" | custom-call | flops 6442450944 | bytes 10000000 | tf_op jit(solution)/shard_map/cross_backward/pallas_call | solution.py:765
  137.8 26.6 %self_backward.1 = (f32[768,512]{1,0:T(8,128)}, f32[128,512]{1,0:T(8,128)}, f32[2,512]{1,0:T(2,128)}, bf16[2,2,4,128,256]{4,3,2,1,0:T(8,128)(2,1)}, bf16[2,2,4,128,256]{4,3,2,1,0:T(8,128)(2,1)}) custom-call(s32[4]{0:T(128)} %pad_add_fusion.meta, s32[2,24]{1,0:T(2,128)} %add_select_fusion.segs, bf16[1536,512]{1,0:T(8,128)(2,1)} %bitcast.187, ...), custom_call_target="tpu_custom_call" | custom-call | flops 6442450944 | bytes 10000000 | tf_op jit(solution)/shard_map/self_backward/pallas_call | solution.py:789
  171.3 11.5 %collective-permute-start.67 = (f32[8,512]{1,0:T(8,128)S(1)}, f32[8,512]{1,0:T(8,128)S(1)}, u32[]{:S(2)}, u32[]{:S(2)}) collective-permute-start(f32[8,512]{1,0:T(8,128)S(1)} %add.214), channel_id=1, source_target_pairs={{0,2},{2,0},{4,6},{6,4},{8,10},{10,8},{12,14},{14,12},{1,3},{3,1},... | collective-permute-start | bytes 49160 | tf_op jit(solution)/shard_map/ppermute | solution.py:609
  202.7 5.5 %collective-permute-done.55 = bf16[2,4,64,512]{3,2,1,0:T(8,128)(2,1)S(1)} collective-permute-done((bf16[2,4,64,512]{3,2,1,0:T(8,128)(2,1)S(1)}, bf16[2,4,64,512]{3,2,1,0:T(8,128)(2,1)S(1)}, u32[]{:S(2)}, u32[]{:S(2)}) %collective-permute-start.55) | collective-permute-done | bytes 524320 | tf_op jit(solution)/shard_map/ppermute | solution.py:609
  210.7 8.8 %collective-permute-done.44 = bf16[2,4,128,256]{3,2,1,0:T(8,128)(2,1)S(1)} collective-permute-done((bf16[2,4,128,256]{3,2,1,0:T(8,128)(2,1)S(1)}, bf16[2,4,128,256]{3,2,1,0:T(8,128)(2,1)S(1)}, u32[]{:S(2)}, u32[]{:S(2)}) %collective-permute-start.44) | collective-permute-done | bytes 524320 | tf_op jit(solution)/shard_map/ppermute | solution.py:609
  219.7 11.1 %collective-permute-done.33 = bf16[2,4,128,256]{3,2,1,0:T(8,128)(2,1)S(1)} collective-permute-done((bf16[2,4,128,256]{3,2,1,0:T(8,128)(2,1)S(1)}, bf16[2,4,128,256]{3,2,1,0:T(8,128)(2,1)S(1)}, u32[]{:S(2)}, u32[]{:S(2)}) %collective-permute-start.33) | collective-permute-done | bytes 524320 | tf_op jit(solution)/shard_map/ppermute | solution.py:609
  230.9 11.1 %collective-permute-done.22 = bf16[2,4,128,256]{3,2,1,0:T(8,128)(2,1)S(1)} collective-permute-done((bf16[2,4,128,256]{3,2,1,0:T(8,128)(2,1)S(1)}, bf16[2,4,128,256]{3,2,1,0:T(8,128)(2,1)S(1)}, u32[]{:S(2)}, u32[]{:S(2)}) %collective-permute-start.22) | collective-permute-done | bytes 524320 | tf_op jit(solution)/shard_map/ppermute | solution.py:609
  246.5 4.7 %collective-permute-done.34 = bf16[4,128,256]{2,1,0:T(8,128)(2,1)S(1)} collective-permute-done((bf16[4,128,256]{2,1,0:T(8,128)(2,1)S(1)}, bf16[4,128,256]{2,1,0:T(8,128)(2,1)S(1)}, u32[]{:S(2)}, u32[]{:S(2)}) %collective-permute-start.34) | collective-permute-done | bytes 262176 | tf_op jit(solution)/shard_map/ppermute | solution.py:609
  259.5 3.7 %collective-permute-done.35 = bf16[2,128,256]{2,1,0:T(8,128)(2,1)S(1)} collective-permute-done((bf16[2,128,256]{2,1,0:T(8,128)(2,1)S(1)}, bf16[2,128,256]{2,1,0:T(8,128)(2,1)S(1)}, u32[]{:S(2)}, u32[]{:S(2)}) %collective-permute-start.35) | collective-permute-done | bytes 131104 | tf_op jit(solution)/shard_map/ppermute | solution.py:609
  266.4 2.7 collective-permute-start.25
  269.1 2.8 collective-permute-done.47
  272.0 3.1 collective-permute-start.60
  283.5 2.8 collective-permute-done.37
  313.6 7.7 %collective-permute-done.51.by_x = bf16[4,128,256]{2,1,0:T(8,128)(2,1)S(1)} collective-permute-done((bf16[4,128,256]{2,1,0:T(8,128)(2,1)S(1)}, bf16[4,128,256]{2,1,0:T(8,128)(2,1)S(1)}, u32[]{:S(2)}, u32[]{:S(2)}) %collective-permute-start.51) | collective-permute-done | bytes 262176 | tf_op jit(solution)/shard_map/ppermute | solution.py:609
  322.6 2.9 fusion.1
  325.5 3.3 unpack_mixed.3
  328.8 2.8 reshape.199
  332.4 3.3 unpack_mixed.2
  339.2 3.4 unpack_rows.1
  342.6 3.4 unpack_columns.1
  (274 shorter events, 116.8 us)
Async XLA Ops:
  0.7 33.6 %collective-permute-start.1 = (bf16[1536,512]{1,0:T(8,128)(2,1)}, bf16[1536,512]{1,0:T(8,128)(2,1)}, u32[]{:S(2)}, u32[]{:S(2)}) collective-permute-start(bf16[1536,512]{1,0:T(8,128)(2,1)} %bitcast.183), channel_id=1, source_target_pairs={{0,16},{16,0},{1,17},{17,1},{2,18},{18,2},{3,19},{19,3},{4,20},{20... | collective-permute-start | bytes 4718600 | tf_op jit(solution)/shard_map/ppermute | solution.py:609
  31.6 25.1 %collective-permute-start.8 = (bf16[512,256]{1,0:T(8,128)(2,1)}, bf16[512,256]{1,0:T(8,128)(2,1)S(1)}, u32[]{:S(2)}, u32[]{:S(2)}) collective-permute-start(bf16[512,256]{1,0:T(8,128)(2,1)} %collective-permute-done.6.w1), channel_id=1, source_target_pairs={{0,16},{16,0},{1,17},{17,1},{2,18},{18,2},{3,19},{19,3},{4,20},{20... | collective-permute-start | bytes 786440 | tf_op jit(solution)/shard_map/ppermute | solution.py:609
  32.1 24.7 %collective-permute-start.11 = (bf16[512,256]{1,0:T(8,128)(2,1)S(1)}, bf16[512,256]{1,0:T(8,128)(2,1)S(1)}, u32[]{:S(2)}, u32[]{:S(2)}) collective-permute-start(bf16[512,256]{1,0:T(8,128)(2,1)S(1)} %collective-permute-done.10.i1), channel_id=1, source_target_pairs={{0,2},{2,0},{4,6},{6,4},{8,10},{10,8},{12,14},{14,12},{1,3},{3,1},... | collective-permute-start | bytes 786440 | tf_op jit(solution)/shard_map/ppermute | solution.py:609
  32.3 49.7 %collective-permute-start.12 = (bf16[512,256]{1,0:T(8,128)(2,1)S(1)}, bf16[512,256]{1,0:T(8,128)(2,1)S(1)}, u32[]{:S(2)}, u32[]{:S(2)}) collective-permute-start(bf16[512,256]{1,0:T(8,128)(2,1)S(1)} %collective-permute-done.10.i1), channel_id=1, source_target_pairs={{0,16},{16,0},{1,17},{17,1},{2,18},{18,2},{3,19},{19,3},{4,20},{20... | collective-permute-start | bytes 786440 | tf_op jit(solution)/shard_map/ppermute | solution.py:609
  32.3 25.0 %collective-permute-start.15 = (bf16[256,512]{1,0:T(8,128)(2,1)}, bf16[256,512]{1,0:T(8,128)(2,1)S(1)}, u32[]{:S(2)}, u32[]{:S(2)}) collective-permute-start(bf16[256,512]{1,0:T(8,128)(2,1)} %collective-permute-done.14.o1), channel_id=1, source_target_pairs={{0,2},{2,0},{4,6},{6,4},{8,10},{10,8},{12,14},{14,12},{1,3},{3,1},... | collective-permute-start | bytes 786440 | tf_op jit(solution)/shard_map/ppermute | solution.py:609
  34.2 23.2 %collective-permute-start.9 = (bf16[512,256]{1,0:T(8,128)(2,1)}, bf16[512,256]{1,0:T(8,128)(2,1)S(1)}, u32[]{:S(2)}, u32[]{:S(2)}) collective-permute-start(bf16[512,256]{1,0:T(8,128)(2,1)} %collective-permute-done.7.w2), channel_id=1, source_target_pairs={{0,16},{16,0},{1,17},{17,1},{2,18},{18,2},{3,19},{19,3},{4,20},{20... | collective-permute-start | bytes 786440 | tf_op jit(solution)/shard_map/ppermute | solution.py:609
  56.7 25.3 %collective-permute-start.16 = (bf16[256,512]{1,0:T(8,128)(2,1)}, bf16[256,512]{1,0:T(8,128)(2,1)S(1)}, u32[]{:S(2)}, u32[]{:S(2)}) collective-permute-start(bf16[256,512]{1,0:T(8,128)(2,1)} %collective-permute-done.14.o1), channel_id=1, source_target_pairs={{0,16},{16,0},{1,17},{17,1},{2,18},{18,2},{3,19},{19,3},{4,20},{20... | collective-permute-start | bytes 786440 | tf_op jit(solution)/shard_map/ppermute | solution.py:609
  56.8 25.2 %collective-permute-start.13 = (bf16[512,256]{1,0:T(8,128)(2,1)S(1)}, bf16[512,256]{1,0:T(8,128)(2,1)S(1)}, u32[]{:S(2)}, u32[]{:S(2)}) collective-permute-start(bf16[512,256]{1,0:T(8,128)(2,1)S(1)} %collective-permute-done.11.i2), channel_id=1, source_target_pairs={{0,16},{16,0},{1,17},{17,1},{2,18},{18,2},{3,19},{19,3},{4,20},{20... | collective-permute-start | bytes 786440 | tf_op jit(solution)/shard_map/ppermute | solution.py:609
  57.3 24.7 %collective-permute-start.17 = (bf16[256,512]{1,0:T(8,128)(2,1)S(1)}, bf16[256,512]{1,0:T(8,128)(2,1)S(1)}, u32[]{:S(2)}, u32[]{:S(2)}) collective-permute-start(bf16[256,512]{1,0:T(8,128)(2,1)S(1)} %collective-permute-done.15.o2), channel_id=1, source_target_pairs={{0,16},{16,0},{1,17},{17,1},{2,18},{18,2},{3,19},{19,3},{4,20},{20... | collective-permute-start | bytes 786440 | tf_op jit(solution)/shard_map/ppermute | solution.py:609
  108.1 81.8 %collective-permute-start.54 = (bf16[2,2,4,64,512]{4,3,2,1,0:T(8,128)(2,1)}, bf16[2,2,4,64,512]{4,3,2,1,0:T(8,128)(2,1)}, u32[]{:S(2)}, u32[]{:S(2)}) collective-permute-start(bf16[2,2,4,64,512]{4,3,2,1,0:T(8,128)(2,1)} %get-tuple-element.67), channel_id=1, source_target_pairs={{0,16},{16,0},{1,17},{17,1},{2,18},{18,2},{3,19},{19,3},{4,20},{20... | collective-permute-start | bytes 3145736 | tf_op jit(solution)/shard_map/ppermute | solution.py:609
  108.1 85.5 %collective-permute-start.43 = (bf16[2,2,4,128,256]{4,3,2,1,0:T(8,128)(2,1)}, bf16[2,2,4,128,256]{4,3,2,1,0:T(8,128)(2,1)}, u32[]{:S(2)}, u32[]{:S(2)}) collective-permute-start(bf16[2,2,4,128,256]{4,3,2,1,0:T(8,128)(2,1)} %get-tuple-element.65), channel_id=1, source_target_pairs={{0,16},{16,0},{1,17},{17,1},{2,18},{18,2},{3,19},{19,3},{4,20},{20... | collective-permute-start | bytes 3145736 | tf_op jit(solution)/shard_map/ppermute | solution.py:609
  137.7 59.7 %collective-permute-start.32 = (bf16[2,2,4,128,256]{4,3,2,1,0:T(8,128)(2,1)}, bf16[2,2,4,128,256]{4,3,2,1,0:T(8,128)(2,1)}, u32[]{:S(2)}, u32[]{:S(2)}) collective-permute-start(bf16[2,2,4,128,256]{4,3,2,1,0:T(8,128)(2,1)} %get-tuple-element.60), channel_id=1, source_target_pairs={{0,16},{16,0},{1,17},{17,1},{2,18},{18,2},{3,19},{19,3},{4,20},{20... | collective-permute-start | bytes 3145736 | tf_op jit(solution)/shard_map/ppermute | solution.py:609
  164.5 34.6 %collective-permute-start.21 = (bf16[2,2,4,128,256]{4,3,2,1,0:T(8,128)(2,1)}, bf16[2,2,4,128,256]{4,3,2,1,0:T(8,128)(2,1)}, u32[]{:S(2)}, u32[]{:S(2)}) collective-permute-start(bf16[2,2,4,128,256]{4,3,2,1,0:T(8,128)(2,1)} %get-tuple-element.56), channel_id=1, source_target_pairs={{0,16},{16,0},{1,17},{17,1},{2,18},{18,2},{3,19},{19,3},{4,20},{20... | collective-permute-start | bytes 3145736 | tf_op jit(solution)/shard_map/ppermute | solution.py:609
  188.2 118.7 %collective-permute-start.20 = (bf16[1536,512]{1,0:T(8,128)(2,1)S(1)}, bf16[1536,512]{1,0:T(8,128)(2,1)S(1)}, u32[]{:S(2)}, u32[]{:S(2)}) collective-permute-start(bf16[1536,512]{1,0:T(8,128)(2,1)S(1)} %copy-done.4), channel_id=1, source_target_pairs={{16,0},{17,1},{18,2},{19,3},{20,4},{21,5},{22,6},{23,7},{24,8},{25... | collective-permute-start | bytes 4718600 | tf_op jit(solution)/shard_map/ppermute | solution.py:845
  189.8 82.1 %collective-permute-start.69 = (f32[8,512]{1,0:T(8,128)S(1)}, f32[8,512]{1,0:T(8,128)S(1)}, u32[]{:S(2)}, u32[]{:S(2)}) collective-permute-start(f32[8,512]{1,0:T(8,128)S(1)} %add.216), channel_id=1, source_target_pairs={{0,8},{2,10},{4,12},{6,14},{8,0},{10,2},{12,4},{14,6},{1,9},{3,11}... | collective-permute-start | bytes 49160 | tf_op jit(solution)/shard_map/ppermute | solution.py:609
  197.4 22.1 %collective-permute-start.44 = (bf16[2,4,128,256]{3,2,1,0:T(8,128)(2,1)S(1)}, bf16[2,4,128,256]{3,2,1,0:T(8,128)(2,1)S(1)}, u32[]{:S(2)}, u32[]{:S(2)}) collective-permute-start(bf16[2,4,128,256]{3,2,1,0:T(8,128)(2,1)S(1)} %get-tuple-element.100), channel_id=1, source_target_pairs={{0,1},{1,0},{2,3},{3,2},{4,5},{5,4},{6,7},{7,6},{8,9},{9,8},{10,11... | collective-permute-start | bytes 1572872 | tf_op jit(solution)/shard_map/ppermute | solution.py:609
  199.1 31.6 %collective-permute-start.33 = (bf16[2,4,128,256]{3,2,1,0:T(8,128)(2,1)S(1)}, bf16[2,4,128,256]{3,2,1,0:T(8,128)(2,1)S(1)}, u32[]{:S(2)}, u32[]{:S(2)}) collective-permute-start(bf16[2,4,128,256]{3,2,1,0:T(8,128)(2,1)S(1)} %get-tuple-element.102), channel_id=1, source_target_pairs={{0,1},{1,0},{2,3},{3,2},{4,5},{5,4},{6,7},{7,6},{8,9},{9,8},{10,11... | collective-permute-start | bytes 1572872 | tf_op jit(solution)/shard_map/ppermute | solution.py:609
  208.3 33.7 %collective-permute-start.22 = (bf16[2,4,128,256]{3,2,1,0:T(8,128)(2,1)S(1)}, bf16[2,4,128,256]{3,2,1,0:T(8,128)(2,1)S(1)}, u32[]{:S(2)}, u32[]{:S(2)}) collective-permute-start(bf16[2,4,128,256]{3,2,1,0:T(8,128)(2,1)S(1)} %get-tuple-element.104), channel_id=1, source_target_pairs={{0,1},{1,0},{2,3},{3,2},{4,5},{5,4},{6,7},{7,6},{8,9},{9,8},{10,11... | collective-permute-start | bytes 1572872 | tf_op jit(solution)/shard_map/ppermute | solution.py:609
  219.5 22.6 %collective-permute-start.56 = (bf16[4,64,512]{2,1,0:T(8,128)(2,1)S(1)}, bf16[4,64,512]{2,1,0:T(8,128)(2,1)S(1)}, u32[]{:S(2)}, u32[]{:S(2)}) collective-permute-start(bf16[4,64,512]{2,1,0:T(8,128)(2,1)S(1)} %get-tuple-element.106), channel_id=1, source_target_pairs={{0,2},{2,0},{4,6},{6,4},{8,10},{10,8},{12,14},{14,12},{1,3},{3,1},... | collective-permute-start | bytes 786440 | tf_op jit(solution)/shard_map/ppermute | solution.py:609
  278.2 27.2 %collective-permute-start.19 = (bf16[768,512]{1,0:T(8,128)(2,1)S(1)}, bf16[768,512]{1,0:T(8,128)(2,1)S(1)}, u32[]{:S(2)}, u32[]{:S(2)}) collective-permute-start(bf16[768,512]{1,0:T(8,128)(2,1)S(1)} %convert_element_type.496), channel_id=1, source_target_pairs={{0,16},{1,17},{2,18},{3,19},{4,20},{5,21},{6,22},{7,23},{8,24},{9,... | collective-permute-start | bytes 2359304 | tf_op jit(solution)/shard_map/ppermute | solution.py:844
  279.6 26.0 %collective-permute-start.18 = (bf16[768,512]{1,0:T(8,128)(2,1)S(1)}, bf16[768,512]{1,0:T(8,128)(2,1)S(1)}, u32[]{:S(2)}, u32[]{:S(2)}) collective-permute-start(bf16[768,512]{1,0:T(8,128)(2,1)S(1)} %copy-done.13), channel_id=1, source_target_pairs={{0,16},{1,17},{2,18},{3,19},{4,20},{5,21},{6,22},{7,23},{8,24},{9,... | collective-permute-start | bytes 2359304 | tf_op jit(solution)/shard_map/ppermute | solution.py:843
  321.3 17.9 %collective-permute-start.63 = (bf16[4,64,512]{2,1,0:T(8,128)(2,1)S(1)}, bf16[4,64,512]{2,1,0:T(8,128)(2,1)}, u32[]{:S(2)}, u32[]{:S(2)}) collective-permute-start(bf16[4,64,512]{2,1,0:T(8,128)(2,1)S(1)} %pad_maximum_fusion.5.mine), channel_id=1, source_target_pairs={{0,16},{16,0},{1,17},{17,1},{2,18},{18,2},{3,19},{19,3},{4,20},{20... | collective-permute-start | bytes 786440 | tf_op jit(solution)/shard_map/ppermute | solution.py:609
  321.4 21.2 %collective-permute-start.52 = (bf16[4,128,256]{2,1,0:T(8,128)(2,1)S(1)}, bf16[4,128,256]{2,1,0:T(8,128)(2,1)}, u32[]{:S(2)}, u32[]{:S(2)}) collective-permute-start(bf16[4,128,256]{2,1,0:T(8,128)(2,1)S(1)} %pad_maximum_fusion.4.mine), channel_id=1, source_target_pairs={{0,16},{16,0},{1,17},{17,1},{2,18},{18,2},{3,19},{19,3},{4,20},{20... | collective-permute-start | bytes 786440 | tf_op jit(solution)/shard_map/ppermute | solution.py:609
  322.0 20.6 %collective-permute-start.53 = (bf16[4,128,256]{2,1,0:T(8,128)(2,1)S(1)}, bf16[4,128,256]{2,1,0:T(8,128)(2,1)}, u32[]{:S(2)}, u32[]{:S(2)}) collective-permute-start(bf16[4,128,256]{2,1,0:T(8,128)(2,1)S(1)} %collective-permute-done.51.by_x), channel_id=1, source_target_pairs={{0,16},{16,0},{1,17},{17,1},{2,18},{18,2},{3,19},{19,3},{4,20},{20... | collective-permute-start | bytes 786440 | tf_op jit(solution)/shard_map/ppermute | solution.py:609
  (87 other events, 835.8 us)
